TPU v7x, 512 devices: a whole 4x4x16 slice. The times are simulated.
512 devices in a mesh: ctx: 64 (over z, x), tp: 8 (over y, core).
Axes of the slice: x: 4, y: 4, z: 16, core: 2. Of those that a mesh axis runs over, the one named last changes fastest.
Arguments:
- new_hidden: bfloat16 [3, 4, 8192], P(None, None, 'ctx'), may hold values from -40 to 40
- norm_gain: float32 [8192], P('ctx'), may hold values from 0.5 to 1.5
- qkv_weight: bfloat16 [8192, 8, 1280], P('ctx', 'tp'), may hold values from -0.0625 to 0.0625
- out_weight: bfloat16 [8, 1024, 8192], P('tp', None, 'ctx'), may hold values from -0.0625 to 0.0625
- owned_cache: bfloat16 [8192, 16, 8, 256], P('ctx', None, 'tp'), may hold values from -128 to 128, as said below
- lengths: int32 [4], replicated, may hold values from 1 to 32768, as said below
- owner_device: int32 [64], replicated, may hold values from 0 to 63, each once
- block_target: int32 [8192, 1], replicated, may hold values from 0 to 63; in each aligned block of 128 rows (0 to 127, 128 to 255, ...) at most 2 rows name the same one
Outputs:
- attended: bfloat16 [3, 4, 8192], P(None, None, 'ctx')
- relaid_cache: bfloat16 [8192, 16, 8, 256], P('ctx', None, 'tp')
Inputs may be any that keep to these rules, and one draw needn't show every extreme that they name: `owned_cache`: keys fill the first 128 entries of the last dimension, values the rest; entries past a sequence's length are not read. `lengths`: one sequence has exactly 32768 cached tokens; another has at most 8. `owner_device`: each device holds exactly one segment. `block_target`: among the 128 rows of each device every device number stands exactly 2 times.
All inputs are finite; a program needn't handle non-finite values.
Results may differ from a plain program's by a relative error of at most 0.01705.
The roundings to bfloat16 on the way count: a program that leaves them out, or rounds other values in their place, can miss the bound.
Values may be sent and summed in bfloat16 or wider, within the bound.
A program may use at most 64 MiB of HBM per device.

v0:
```python
import math

import jax
import jax.numpy as jnp
from jax import lax
from jax.sharding import PartitionSpec as P


def rotate(values, position):
    half = values.shape[-1] // 2
    inverse = jnp.exp(
        -math.log(500000.0) * jnp.arange(half, dtype=jnp.float32) * 2.0 / values.shape[-1]
    )
    angle = position[..., None] * inverse
    cosine = jnp.cos(angle)
    sine = jnp.sin(angle)
    first = values[..., :half]
    second = values[..., half:]
    return jnp.concatenate(
        [first * cosine - second * sine, second * cosine + first * sine], axis=-1
    )


def partial_attention(query_rows, cache_rows, live_mask, scale):
    head_dim = query_rows.shape[-1]
    scores = (
        jnp.einsum(
            "skgd,sjkd->skgj",
            query_rows,
            cache_rows[..., :head_dim],
            preferred_element_type=jnp.float32,
        )
        * scale
    )
    scores = jnp.where(live_mask[:, None, None, :], scores, -1e30)
    highest = jnp.max(scores, axis=-1)
    weights = jnp.where(live_mask[:, None, None, :], jnp.exp(scores - highest[..., None]), 0.0)
    total = jnp.sum(weights, axis=-1)
    accumulated = jnp.einsum(
        "skgj,sjkd->skgd",
        weights.astype(jnp.bfloat16),
        cache_rows[..., head_dim:],
        preferred_element_type=jnp.float32,
    )
    return (highest, total, accumulated)


def combine_sources(highest, total, accumulated, seq_of_source, seqs):
    member = seq_of_source[None, :] == jnp.arange(seqs, dtype=jnp.int32)[:, None]
    peak = jnp.max(jnp.where(member[:, :, None, None], highest[None], -1e30), axis=1)
    factor = jnp.exp(highest - peak[seq_of_source])
    member_wide = member.astype(jnp.float32)
    total = jnp.einsum("sn,nkg->skg", member_wide, total * factor, precision=lax.Precision.HIGHEST)
    accumulated = jnp.einsum(
        "sn,nkgd->skgd",
        member_wide,
        accumulated * factor[..., None],
        precision=lax.Precision.HIGHEST,
    )
    return (peak, total, accumulated)


def finish(highest, total, accumulated, fresh_scores, fresh_values):
    peak = jnp.maximum(highest, jnp.max(fresh_scores, axis=-1))
    rescale = jnp.exp(highest - peak)
    fresh_weights = jnp.exp(fresh_scores - peak[..., None])
    total = total * rescale + jnp.sum(fresh_weights, axis=-1)
    accumulated = accumulated * rescale[..., None] + jnp.einsum(
        "skgt,sktd->skgd",
        fresh_weights.astype(jnp.bfloat16),
        fresh_values,
        preferred_element_type=jnp.float32,
    )
    return (accumulated / total[..., None]).astype(jnp.bfloat16)


def body(
    new_hidden, norm_gain, qkv_weight, out_weight, owned_cache, lengths, owner_device, block_target
):
    n_context = lax.axis_size("ctx")
    my_index = lax.axis_index("ctx")
    own_blocks, block_len, heads_local, both_width = owned_cache.shape
    head_dim = both_width // 2
    slots = own_blocks // n_context
    group = qkv_weight.shape[2] // head_dim - 2
    steps_count, seqs, width_local = new_hidden.shape
    model_width = width_local * n_context
    segments = n_context // seqs
    segment_len = own_blocks * block_len
    scale = 1.0 / math.sqrt(head_dim)
    targets = block_target[:, 0].reshape(n_context, own_blocks)
    devices = jnp.arange(n_context, dtype=jnp.int32)
    onehot = (targets[:, :, None] == devices[None, None, :]).astype(jnp.int32)
    ranking = jnp.sum(jnp.cumsum(onehot, axis=1) * onehot, axis=2) - 1
    my_targets = lax.dynamic_index_in_dim(targets, my_index, 0, keepdims=False)
    my_ranks = lax.dynamic_index_in_dim(ranking, my_index, 0, keepdims=False)
    slot_index = my_targets * slots + my_ranks
    outgoing = jnp.zeros_like(owned_cache).at[slot_index].set(owned_cache)
    relaid = lax.all_to_all(
        outgoing.reshape(n_context, slots, block_len, heads_local, both_width),
        "ctx",
        split_axis=0,
        concat_axis=0,
        tiled=True,
    )
    ranks_here = jnp.where(targets == my_index, ranking, -1)
    picks = (ranks_here[:, :, None] == jnp.arange(slots, dtype=jnp.int32)[None, None, :]).astype(
        jnp.int32
    )
    block_number = jnp.sum(picks * jnp.arange(own_blocks, dtype=jnp.int32)[None, :, None], axis=1)
    holder = (owner_device[None, :] == devices[:, None]).astype(jnp.int32)
    segment_of_device = jnp.sum(holder * devices[None, :], axis=1)
    seq_of_device = segment_of_device // segments
    offset_of_device = segment_of_device % segments * segment_len
    length_of_device = lengths[seq_of_device]
    token_place = (
        offset_of_device[:, None, None]
        + block_number[:, :, None] * block_len
        + jnp.arange(block_len, dtype=jnp.int32)[None, None, :]
    ).reshape(n_context, slots * block_len)
    live_relaid = token_place < length_of_device[:, None]
    relaid_rows = relaid.reshape(n_context, slots * block_len, heads_local, both_width)
    weight_flat = qkv_weight.reshape(width_local, -1)
    out_flat = out_weight.reshape(-1, width_local)
    new_keys = []
    new_values = []
    results = []
    for decode_step in range(steps_count):
        hidden = new_hidden[decode_step]
        scaled = (hidden.astype(jnp.float32) * norm_gain).astype(jnp.bfloat16)
        partial_proj = jnp.dot(scaled, weight_flat, preferred_element_type=jnp.float32)
        squares = jnp.sum(jnp.square(hidden.astype(jnp.float32)), axis=1)
        partial_proj, squares = lax.psum((partial_proj, squares), "ctx")
        projected = partial_proj / jnp.sqrt(squares / model_width + 1e-05)[:, None]
        projected = projected.reshape(seqs, heads_local, group + 2, head_dim)
        position = lengths.astype(jnp.float32) + decode_step
        queries = rotate(projected[:, :, :group], position[:, None, None]).astype(jnp.bfloat16)
        new_keys.append(rotate(projected[:, :, group], position[:, None]).astype(jnp.bfloat16))
        new_values.append(projected[:, :, group + 1].astype(jnp.bfloat16))
        fresh_keys = jnp.stack(new_keys, 2)
        fresh_values = jnp.stack(new_values, 2)
        fresh_scores = (
            jnp.einsum("skgd,sktd->skgt", queries, fresh_keys, preferred_element_type=jnp.float32)
            * scale
        )
        slot_queries = queries[seq_of_device]
        highest, total, accumulated = partial_attention(
            slot_queries, relaid_rows, live_relaid, scale
        )
        highest, total, accumulated = combine_sources(
            highest, total, accumulated, seq_of_device, seqs
        )
        overall = lax.pmax(highest, "ctx")
        factor = jnp.exp(highest - overall)
        total, accumulated = lax.psum((total * factor, accumulated * factor[..., None]), "ctx")
        highest = overall
        attention = finish(highest, total, accumulated, fresh_scores, fresh_values)
        mixed = jnp.dot(attention.reshape(seqs, -1), out_flat, preferred_element_type=jnp.float32)
        mixed = lax.psum(mixed, "tp")
        results.append(mixed.astype(jnp.bfloat16))
    return (
        jnp.stack(results, 0),
        relaid.reshape(n_context * slots, block_len, heads_local, both_width),
    )


def solution(mesh):
    in_specs = (
        P(None, None, "ctx"),
        P("ctx"),
        P("ctx", "tp", None),
        P("tp", None, "ctx"),
        P("ctx", None, "tp", None),
        P(),
        P(),
        P(),
    )
    out_specs = (P(None, None, "ctx"), P("ctx", None, "tp", None))
    return jax.shard_map(body, mesh=mesh, in_specs=in_specs, out_specs=out_specs, check_vma=False)
```

profile of v0, /device:TPU:24, one launch (start us, length us, event | category | flops | bytes accessed | tf_op | source)
XLA Modules:
  0.0 798.6 jit_solution(1623992772300459188)
XLA Ops:
  0.7 1.0 copy.294
  1.6 4.4 select_reduce_fusion
  6.2 1.0 broadcast.688
  7.3 13.7 %scatter_fusion = bf16[128,16,256]{2,1,0:T(8,128)(2,1)} fusion(bf16[128,16,256]{2,1,0:T(8,128)(2,1)} %broadcast.688, s32[128]{0:T(128)S(1)} %fusion.168, bf16[128,16,256]{2,1,0:T(8,128)(2,1)S(1)} %bitcast.294), kind=kCustom, calls=%fused_computation.6 | custom fusion | bytes 3146240 | tf_op jit(solution)/shard_map/scatter | solution.py:98
  21.0 18.7 %all-to-all-start = ((bf16[64,2,16,1,256]{4,2,1,3,0:T(8,128)(2,1)}), bf16[64,2,16,1,256]{4,2,1,3,0:T(8,128)(2,1)S(1)}, u32[]{:S(2)}, u32[]{:S(2)}) async-start(bf16[64,2,16,1,256]{4,2,1,3,0:T(8,128)(2,1)} %bitcast.14), calls=%async_computation | async-start | bytes 2097152 | tf_op jit(solution)/shard_map/all_to_all | solution.py:99
  40.4 314.6 %all-reduce.1 = (f32[4,1280]{1,0:T(4,128)S(1)}, f32[4]{0:T(128)S(1)}, f32[4,1280]{1,0:T(4,128)S(1)}, f32[4]{0:T(128)S(1)}, f32[4,1280]{1,0:T(4,128)S(1)}, /*index=5*/f32[4]{0:T(128)S(1)}) all-reduce(f32[4,1280]{1,0:T(4,128)S(1)} %fusion.12, f32[4]{0:T(128)S(1)} %get-tuple-element.13, ...), channel_id=1, replica_groups=mesh['ctx'=64,'tp'=8] {'ctx'}, use_global_device_ids=true, to_apply=%region_27.28 | all-reduce | flops 15372 | bytes 122976 | tf_op jit(solution)/shard_map/psum | solution.py:133
  355.7 0.7 fusion.182
  356.7 2.5 and_select_fusion.2
  359.7 0.6 gather_fusion
  360.5 0.6 gather_fusion.2
  361.3 0.6 gather_fusion.4
  362.2 0.2 fusion.186
  362.6 0.5 fusion.183
  363.2 0.5 fusion.184
  363.7 0.5 fusion.185
  364.3 0.6 gather_fusion.5
  364.9 0.6 gather_fusion.3
  365.5 0.6 gather_fusion.1
  366.1 140.1 %all-reduce.2 = (f32[4,1,8]{2,0,1:T(4,128)S(1)}, f32[4,1,8]{2,0,1:T(4,128)S(1)}, f32[4,1,8]{2,0,1:T(4,128)S(1)}) all-reduce(f32[4,1,8]{2,0,1:T(4,128)S(1)} %bitcast.286, f32[4,1,8]{2,0,1:T(4,128)S(1)} %bitcast.285, f32[4,1,8]{2,0,1:T(4,128)S(1)} %bitcast.284), channel_id=1, replica_groups=mesh['ctx'=64,'tp'=8] {'ctx'}, use_global_device_ids=true, to_apply=%region_32.33 | all-reduce | flops 96 | bytes 768 | tf_op jit(solution)/shard_map/pmax | solution.py:153
  506.8 0.3 convolution_multiply_fusion
  507.1 0.5 fusion.27
  507.8 0.3 convolution_multiply_fusion.2
  508.4 0.3 convolution_multiply_fusion.4
  508.9 0.2 fusion.6
  509.2 0.2 fusion.7
  509.4 0.2 fusion.8
  509.6 275.9 %all-reduce = (f32[4,1,8,128]{3,0,2,1:T(4,128)S(1)}, f32[4,1,8]{2,0,1:T(4,128)S(1)}, f32[4,1,8,128]{3,0,2,1:T(4,128)S(1)}, f32[4,1,8]{2,0,1:T(4,128)S(1)}, f32[4...) all-reduce(f32[4,1,8,128]{3,0,2,1:T(4,128)S(1)} %fusion.6, ...), channel_id=1, replica_groups=mesh['ctx'=64,'tp'=8] {'ctx'}, use_global_device_ids=true, to_apply=%region_33.34 | all-reduce | flops 12384 | bytes 99072 | tf_op jit(solution)/shard_map/psum | solution.py:155
  786.1 0.2 fusion.18
  786.4 0.2 fusion.20
  786.8 10.2 %all-reduce.3 = (bf16[4,128]{1,0:T(4,128)(2,1)S(1)}, bf16[4,128]{1,0:T(4,128)(2,1)S(1)}, bf16[4,128]{1,0:T(4,128)(2,1)S(1)}) all-reduce(f32[4,128]{1,0:T(4,128)S(1)} %fusion.18, f32[4,128]{1,0:T(4,128)S(1)} %fusion.20, f32[4,128]{1,0:T(4,128)S(1)} %fusion.22), channel_id=1, replica_groups=mesh['ctx'=64,'tp'=8] {'tp'}, use_global_device_ids=true, to_apply=%region_38.39 | all-reduce | flops 1536 | bytes 9216 | tf_op jit(solution)/shard_map/psum | solution.py:159
  797.0 0.6 pad_maximum_fusion.2
  797.6 1.0 copy.350
  (98 shorter events, 5.2 us)
Async XLA Ops:
  0.6 39.3 %copy-start = (bf16[128,1,1280]{2,0,1:T(8,128)(2,1)S(1)}, bf16[128,1,1280]{2,0,1:T(8,128)(2,1)}, u32[]{:S(2)}) copy-start(bf16[128,1,1280]{2,0,1:T(8,128)(2,1)} %param.10) | copy-start | bytes 983044
  0.6 6.7 copy-start.1
  21.0 18.7 %copy-start.2 = (bf16[3,4,128]{2,1,0:T(4,128)(2,1)S(1)}, bf16[3,4,128]{2,1,0:T(4,128)(2,1)}, u32[]{:S(2)}) copy-start(bf16[3,4,128]{2,1,0:T(4,128)(2,1)} %param.8) | copy-start | bytes 9220
  21.0 18.9 %copy-start.4 = (f32[128]{0:T(128)S(1)}, f32[128]{0:T(128)}, u32[]{:S(2)}) copy-start(f32[128]{0:T(128)} %param.9) | copy-start | bytes 1540
  21.0 341.6 %all-to-all-start = ((bf16[64,2,16,1,256]{4,2,1,3,0:T(8,128)(2,1)}), bf16[64,2,16,1,256]{4,2,1,3,0:T(8,128)(2,1)S(1)}, u32[]{:S(2)}, u32[]{:S(2)}) async-start(bf16[64,2,16,1,256]{4,2,1,3,0:T(8,128)(2,1)} %bitcast.14), calls=%async_computation | async-start | bytes 2097152 | tf_op jit(solution)/shard_map/all_to_all | solution.py:99
  39.7 315.4 %copy-start.3 = (s32[4]{0:T(128)S(1)}, s32[4]{0:T(128)}, u32[]{:S(2)}) copy-start(s32[4]{0:T(128)} %param.13) | copy-start | bytes 52
  39.7 316.7 %copy-start.6 = (s32[64]{0:T(128)S(1)}, s32[64]{0:T(128)}, u32[]{:S(2)}) copy-start(s32[64]{0:T(128)} %param.14) | copy-start | bytes 772
  508.4 277.8 %copy-start.5 = (bf16[1,1024,128]{2,1,0:T(8,128)(2,1)S(1)}, bf16[1,1024,128]{2,1,0:T(8,128)(2,1)}, u32[]{:S(2)}) copy-start(bf16[1,1024,128]{2,1,0:T(8,128)(2,1)} %param.11) | copy-start | bytes 786436
where the time goes:
time: 803 us; the launch traced here: 799 us
  blocking collectives  741 us (92%)
  local copies, waits for them, and re-layouts  22.5 us (3%)
  starting transfers between devices  18.7 us (2%)
  other arithmetic  10 us (1%)
    psum x1, blocking collectives, body(): partial_proj, squares = lax.psum((partial_proj, squares), 'ctx')  315 us
    psum x1, blocking collectives, body(): lax.psum((total * factor, accumulated * factor[..., None]), 'ctx')  276 us
    pmax x1, blocking collectives, body(): overall = lax.pmax(highest, 'ctx')  140 us
    all_to_all x1, starting transfers between devices, body(): lax.all_to_all(outgoing.reshape(n_context, slots, block_len, heads_local,...  18.7 us
  transfers between devices with their start and end apart: 1, of which 0 were waited for; matrix products, arithmetic and copies ran while one was open for 1% of the time, Pallas kernels for 0%

commit v1 on v0

v1 whole, which is shorter than its diff:
```python
import functools
import math

import jax
import jax.numpy as jnp
import numpy as np
from jax import lax
from jax.experimental import pallas as pl
from jax.experimental.pallas import tpu as pltpu
from jax.sharding import PartitionSpec as P

MESH = pl.DeviceIdType.MESH
ZN, XN, TP = 16, 4, 8
HEADS = 8
LOW = -1e30


def remote(src, dst, send, recv, target):
    return pltpu.make_async_remote_copy(
        src_ref=src,
        dst_ref=dst,
        send_sem=send,
        recv_sem=recv,
        device_id=target,
        device_id_type=MESH,
    )


def wait_bytes(ref, sem):
    pltpu.make_async_copy(ref, ref, sem).wait()


def swap_halves(values, axis):
    return pltpu.roll(values, 64, axis)


def kernel(
    hid_ref, gain_ref, inv_ref, len_ref, own_ref, tgt_hbm, wq_hbm, wo_hbm, cache_hbm,
    att_ref, rel_ref,
    tgt, slot_v, slot_s, wq, wo, cache, packed,
    hid32, pbuf, zbuf, xsend, xbuf, asend, gbuf, kvs,
    bbuf, zb2, x2send, x2buf, ats, agb, osend, tbuf, fs,
    in_sem, own_sem, a2a_send, a2a_recv, chain_send, chain_recv,
):
    me = lax.axis_index("ctx")
    mt = lax.axis_index("tp")
    z = me // XN
    x = me % XN

    def at_z(dz):
        return ((z + dz) % ZN) * XN + x

    def at_x(dx):
        return z * XN + (x + dx) % XN

    barrier = pltpu.get_barrier_semaphore()

    def greet_ctx(k, carry):
        pl.semaphore_signal(barrier, inc=1, device_id={"ctx": (me + k) % (ZN * XN)}, device_id_type=MESH)
        return carry

    def greet_tp(k, carry):
        pl.semaphore_signal(barrier, inc=1, device_id={"tp": (mt + k) % TP}, device_id_type=MESH)
        return carry

    lax.fori_loop(1, ZN * XN, greet_ctx, 0)
    lax.fori_loop(1, TP, greet_tp, 0)

    cp_tgt = pltpu.make_async_copy(tgt_hbm.at[me], tgt, in_sem.at[0])
    cp_wq = pltpu.make_async_copy(wq_hbm, wq, in_sem.at[1])
    cp_cache = pltpu.make_async_copy(cache_hbm, cache, in_sem.at[2])
    cp_wo = pltpu.make_async_copy(wo_hbm, wo, in_sem.at[3])
    cp_tgt.start()
    cp_wq.start()
    cp_cache.start()
    cp_wo.start()

    hid32[...] = jnp.zeros_like(hid32)
    for step in range(3):
        hid32[4 * step : 4 * step + 4, :] = hid_ref[step].astype(jnp.float32)
    hidden = hid32[...]
    scaled = (hidden * gain_ref[...]).astype(jnp.bfloat16)
    row16 = lax.broadcasted_iota(jnp.int32, (16, 128), 0)
    lane16 = lax.broadcasted_iota(jnp.int32, (16, 128), 1)
    squares = jnp.sum(hidden * hidden, axis=1, keepdims=True)
    square_row = jnp.sum(jnp.where(row16 == lane16, squares, 0.0), axis=0, keepdims=True)
    row8 = lax.broadcasted_iota(jnp.int32, (8, 128), 0)
    lane8 = lax.broadcasted_iota(jnp.int32, (8, 128), 1)
    pbuf[120:128, :] = jnp.where(row8 == 0, square_row, 0.0)
    cp_wq.wait()
    for head in range(HEADS + 2):
        part = jnp.dot(
            scaled, wq[:, 128 * head : 128 * head + 128], preferred_element_type=jnp.float32
        )
        pbuf[12 * head : 12 * head + 12, :] = part[0:12, :]

    cp_tgt.wait()
    t_iota = lax.broadcasted_iota(jnp.int32, (64, 128), 0)
    b_iota = lax.broadcasted_iota(jnp.int32, (64, 128), 1)
    match = tgt[...] == t_iota
    first = jnp.min(jnp.where(match, b_iota, 127), axis=1, keepdims=True)
    last = jnp.max(jnp.where(match, b_iota, 0), axis=1, keepdims=True)
    slot_v[...] = jnp.where(b_iota == 0, first, last)
    cp_slot = pltpu.make_async_copy(slot_v, slot_s, in_sem.at[4])
    cp_slot.start()
    cp_slot.wait()
    cp_cache.wait()

    def pack(t, carry):
        packed[2 * t] = cache[slot_s[t, 0]]
        packed[2 * t + 1] = cache[slot_s[t, 1]]
        return carry

    lax.fori_loop(0, ZN * XN, pack, 0)
    mine = pl.ds(2 * me, 2)
    cp_own = pltpu.make_async_copy(packed.at[mine], rel_ref.at[mine], own_sem)
    cp_own.start()

    row24 = lax.broadcasted_iota(jnp.int32, (24, 128), 0)
    lane24 = lax.broadcasted_iota(jnp.int32, (24, 128), 1)
    seq24 = row24 % 4
    row_in = row24 % 12
    length24 = jnp.where(
        seq24 == 0,
        len_ref[0],
        jnp.where(seq24 == 1, len_ref[1], jnp.where(seq24 == 2, len_ref[2], len_ref[3])),
    )
    position = length24.astype(jnp.float32) + (row_in // 4).astype(jnp.float32)
    angle = position * inv_ref[...]
    cosine = jnp.cos(angle)
    sine = jnp.where(lane24 < 64, -jnp.sin(angle), jnp.sin(angle))

    own_iota = lax.broadcasted_iota(jnp.int32, (1, 64), 1)
    segment = jnp.sum(jnp.where(own_ref[...] == me, own_iota, 0), axis=1, keepdims=True)
    my_seq = segment // 16
    my_offset = segment % 16 * 2048
    my_length = jnp.where(
        my_seq == 0,
        len_ref[0],
        jnp.where(my_seq == 1, len_ref[1], jnp.where(my_seq == 2, len_ref[2], len_ref[3])),
    )

    pl.semaphore_wait(barrier, ZN * XN - 1 + TP - 1)

    def send_blocks(dzs, low, high):
        def one(dx, carry):
            for dz in dzs:
                to = ((z + dz + ZN) % ZN) * XN + (x + dx) % XN
                remote(
                    packed.at[pl.ds(2 * to, 2)], rel_ref.at[mine], a2a_send, a2a_recv, {"ctx": to}
                ).start()
            return carry

        lax.fori_loop(low, high, one, 0)

    def scatter_a(dz, carry):
        to = (z + dz) % ZN
        remote(
            pbuf.at[pl.ds(pl.multiple_of(8 * to, 8), 8)], zbuf.at[z],
            chain_send.at[0], chain_recv.at[0], {"ctx": to * XN + x},
        ).start()
        return carry

    lax.fori_loop(1, ZN, scatter_a, 0)
    send_blocks(A2A_PLAN[0][0], *A2A_PLAN[0][1])
    zbuf[z] = pbuf[pl.ds(pl.multiple_of(8 * z, 8), 8), :]
    wait_bytes(zbuf.at[pl.ds(0, ZN - 1)], chain_recv.at[0])
    total = jnp.sum(zbuf[...], axis=0)
    xsend[...] = total
    xbuf[x] = total
    for dx in range(1, XN):
        remote(
            xsend, xbuf.at[x], chain_send.at[1], chain_recv.at[1], {"ctx": at_x(dx)}
        ).start()
    wait_bytes(xbuf.at[pl.ds(0, XN - 1)], chain_recv.at[1])
    total = jnp.sum(xbuf[...], axis=0)
    asend[...] = total
    gbuf[z] = total

    def gather_a(dz, carry):
        remote(
            asend, gbuf.at[z], chain_send.at[2], chain_recv.at[2], {"ctx": at_z(dz)}
        ).start()
        return carry

    lax.fori_loop(1, ZN, gather_a, 0)
    send_blocks(A2A_PLAN[1][0], *A2A_PLAN[1][1])
    wait_bytes(gbuf.at[pl.ds(0, ZN - 1)], chain_recv.at[2])

    whole = gbuf[...].reshape(128, 128)
    square_sum = jnp.sum(
        jnp.where(lane24 == row_in, whole[120:121, :], 0.0), axis=1, keepdims=True
    )
    norm = jnp.sqrt(square_sum / 8192.0 + 1e-05)
    rotated = []
    for g in range(5):
        plain = whole[24 * g : 24 * g + 24, :] / norm
        turned = plain * cosine + swap_halves(plain, 1) * sine
        if g < 4:
            rotated.append(turned)
        else:
            kvs[0:24, :] = jnp.where(row24 < 12, turned, plain)
    kvs[24:32, :] = jnp.zeros((8, 128), jnp.float32)
    queries = jnp.concatenate(rotated, axis=0).astype(jnp.bfloat16)

    pick_row = lax.broadcasted_iota(jnp.int32, (64, 96), 0)
    pick_col = lax.broadcasted_iota(jnp.int32, (64, 96), 1)
    in_tile = pick_row % 8
    tile_step = jnp.where(in_tile >= 3, in_tile - 3, in_tile)
    wanted = 12 * (pick_row // 8) + 4 * tile_step + my_seq
    pick = jnp.where((wanted == pick_col) & (in_tile < 6), 1.0, 0.0).astype(jnp.bfloat16)
    my_queries = jnp.dot(pick, queries, preferred_element_type=jnp.float32).astype(jnp.bfloat16)
    keys = cache[:, :, 0:128].reshape(2048, 128)
    values = cache[:, :, 128:256].reshape(2048, 128)
    scale = 1.0 / math.sqrt(128)
    scores = (
        lax.dot_general(
            my_queries, keys, (((1,), (1,)), ((), ())), preferred_element_type=jnp.float32
        )
        * scale
    )
    place = my_offset + lax.broadcasted_iota(jnp.int32, (1, 2048), 1)
    live = place < my_length
    scores = jnp.where(live, scores, LOW)
    highest = jnp.max(scores, axis=1, keepdims=True)
    weights = jnp.where(live, jnp.exp(scores - highest), 0.0)
    weight_sum = jnp.sum(weights, axis=1, keepdims=True)
    weighted = jnp.dot(weights.astype(jnp.bfloat16), values, preferred_element_type=jnp.float32)
    row64 = lax.broadcasted_iota(jnp.int32, (64, 128), 0) % 8
    lane64 = lax.broadcasted_iota(jnp.int32, (64, 128), 1)
    stats = jnp.where(lane64 < 64, highest, weight_sum)
    bbuf[...] = jnp.where(
        row64 < 3, weighted, jnp.where(row64 < 6, stats, my_seq.astype(jnp.float32))
    )

    head = z % HEADS

    def scatter_b(dz, carry):
        to = (z + dz) % ZN
        remote(
            bbuf.at[pl.ds(pl.multiple_of(8 * (to % HEADS), 8), 8)], zb2.at[z],
            chain_send.at[3], chain_recv.at[3], {"ctx": to * XN + x},
        ).start()
        return carry

    lax.fori_loop(1, ZN, scatter_b, 0)
    send_blocks(A2A_PLAN[2][0], *A2A_PLAN[2][1])
    zb2[z] = bbuf[pl.ds(pl.multiple_of(8 * head, 8), 8), :]

    pick_row = lax.broadcasted_iota(jnp.int32, (16, 96), 0)
    pick_col = lax.broadcasted_iota(jnp.int32, (16, 96), 1)
    wanted = 12 * head + 4 * (pick_row % 3) + pick_row // 3
    pick = jnp.where((wanted == pick_col) & (pick_row < 12), 1.0, 0.0).astype(jnp.bfloat16)
    head_queries = jnp.dot(pick, queries, preferred_element_type=jnp.float32).astype(jnp.bfloat16)
    new_keys = kvs[0:16, :].astype(jnp.bfloat16)
    new_values = kvs[12:28, :].astype(jnp.bfloat16)
    fresh = (
        lax.dot_general(
            head_queries, new_keys, (((1,), (1,)), ((), ())), preferred_element_type=jnp.float32
        )
        * scale
    )
    q_row = lax.broadcasted_iota(jnp.int32, (16, 16), 0)
    k_col = lax.broadcasted_iota(jnp.int32, (16, 16), 1)
    seen = (
        (q_row // 3 == k_col % 4) & (k_col // 4 <= q_row % 3) & (k_col < 12) & (q_row < 12)
    )
    fresh = jnp.where(seen, fresh, LOW)
    fresh_high = jnp.max(fresh, axis=1, keepdims=True)
    x2send[...] = jnp.where(lax.broadcasted_iota(jnp.int32, (32, 128), 0) < 16, 0.0, 1.0)

    wait_bytes(zb2.at[pl.ds(0, ZN - 1)], chain_recv.at[3])
    tiles = zb2[...]
    lane_t = lax.broadcasted_iota(jnp.int32, (16, 8, 128), 2)
    moved = pltpu.roll(tiles, 5, 1)
    turned = swap_halves(moved, 2)
    part_high = jnp.where(lane_t < 64, moved, turned)
    part_sum = jnp.where(lane_t < 64, turned, moved)
    part_seq = tiles[:, 6:7, :]
    for seq in range(4):
        member = part_seq == float(seq)
        high = jnp.max(jnp.where(member, part_high, LOW), axis=0)
        factor = jnp.where(member, jnp.exp(part_high - high[None]), 0.0)
        sums = jnp.sum(factor * part_sum, axis=0)
        accs = jnp.sum(factor * tiles, axis=0)
        both = jnp.where(lane8 < 64, high, sums)
        x2send[3 * seq : 3 * seq + 3, :] = accs[0:3, :]
        x2send[16 + 3 * seq : 16 + 3 * seq + 3, :] = both[0:3, :]
    x2buf[x] = x2send[...]
    for dx in range(1, XN):
        remote(
            x2send, x2buf.at[x], chain_send.at[4], chain_recv.at[4], {"ctx": at_x(dx)}
        ).start()
    send_blocks(A2A_PLAN[3][0], *A2A_PLAN[3][1])
    wait_bytes(x2buf.at[pl.ds(0, XN - 1)], chain_recv.at[4])
    accs = x2buf[:, 0:16, :]
    stats = x2buf[:, 16:32, :]
    lane_x = lax.broadcasted_iota(jnp.int32, (4, 16, 128), 2)
    turned = swap_halves(stats, 2)
    part_high = jnp.where(lane_x < 64, stats, turned)
    part_sum = jnp.where(lane_x < 64, turned, stats)
    high = jnp.maximum(jnp.max(part_high, axis=0), fresh_high)
    factor = jnp.exp(part_high - high[None])
    fresh_weights = jnp.where(seen, jnp.exp(fresh - high[:, 0:1]), 0.0)
    sums = jnp.sum(factor * part_sum, axis=0) + jnp.sum(fresh_weights, axis=1, keepdims=True)
    mixed = jnp.sum(factor * accs, axis=0) + jnp.dot(
        fresh_weights.astype(jnp.bfloat16), new_values, preferred_element_type=jnp.float32
    )
    attention = (mixed / sums).astype(jnp.bfloat16)
    ats[...] = attention
    agb[head] = attention
    for dz in (1, -1, 2, -2, 3, -3, 4):
        remote(
            ats, agb.at[head], chain_send.at[5], chain_recv.at[5], {"ctx": at_z(dz + ZN)}
        ).start()
    send_blocks(A2A_PLAN[4][0], *A2A_PLAN[4][1])
    cp_wo.wait()
    wait_bytes(agb.at[pl.ds(0, HEADS - 1)], chain_recv.at[5])

    out = jnp.zeros((16, 128), jnp.float32)
    for h in range(HEADS):
        out = out + jnp.dot(
            agb[h], wo[128 * h : 128 * h + 128, :], preferred_element_type=jnp.float32
        )
    osend[...] = out
    tbuf[mt] = out
    for dt in range(1, TP):
        remote(
            osend, tbuf.at[mt], chain_send.at[6], chain_recv.at[6], {"tp": (mt + dt) % TP}
        ).start()
    send_blocks(A2A_PLAN[5][0], *A2A_PLAN[5][1])
    wait_bytes(tbuf.at[pl.ds(0, TP - 1)], chain_recv.at[6])
    out = jnp.sum(tbuf[...], axis=0)
    for step in range(3):
        for seq in range(4):
            r = 3 * seq + step
            fs[step, seq : seq + 1, :] = out[r : r + 1, :]
    att_ref[...] = fs[...].astype(jnp.bfloat16)

    wait_bytes(pbuf.at[pl.ds(0, 8 * (ZN - 1))], chain_send.at[0])
    wait_bytes(xbuf.at[pl.ds(0, XN - 1)], chain_send.at[1])
    wait_bytes(gbuf.at[pl.ds(0, ZN - 1)], chain_send.at[2])
    wait_bytes(zb2.at[pl.ds(0, ZN - 1)], chain_send.at[3])
    wait_bytes(x2buf.at[pl.ds(0, XN - 1)], chain_send.at[4])
    wait_bytes(agb.at[pl.ds(0, HEADS - 1)], chain_send.at[5])
    wait_bytes(tbuf.at[pl.ds(0, TP - 1)], chain_send.at[6])
    cp_own.wait()
    others = pl.ds(0, 2 * (ZN * XN - 1))
    wait_bytes(packed.at[others], a2a_send)
    wait_bytes(rel_ref.at[others], a2a_recv)


A2A_PLAN = (
    ((1, -1, 7, -7), (0, 4)),
    ((2, -2, 6, -6), (0, 4)),
    ((3, -3, 5, -5), (0, 4)),
    ((4, -4, 8), (0, 4)),
    ((0,), (1, 4)),
    ((), (0, 0)),
)


def inverse_table():
    half = np.arange(64, dtype=np.float32)
    power = np.float32(-math.log(500000.0)) * half * np.float32(2.0) / np.float32(128.0)
    inverse = np.exp(power.astype(np.float64)).astype(np.float32)
    return np.concatenate([inverse, inverse])[None, :]


def body(
    new_hidden, norm_gain, qkv_weight, out_weight, owned_cache, lengths, owner_device, block_target
):
    f32, bf16, i32 = jnp.float32, jnp.bfloat16, jnp.int32
    vmem = pl.BlockSpec(memory_space=pltpu.VMEM)
    smem = pl.BlockSpec(memory_space=pltpu.SMEM)
    hbm = pl.BlockSpec(memory_space=pl.ANY)
    dma = pltpu.SemaphoreType.DMA
    attended, relaid = pl.pallas_call(
        kernel,
        out_shape=(
            jax.ShapeDtypeStruct((3, 4, 128), bf16),
            jax.ShapeDtypeStruct((128, 16, 256), bf16),
        ),
        in_specs=[vmem, vmem, vmem, smem, vmem, hbm, hbm, hbm, hbm],
        out_specs=(vmem, hbm),
        scratch_shapes=[
            pltpu.VMEM((1, 128), i32),
            pltpu.VMEM((64, 128), i32),
            pltpu.SMEM((64, 128), i32),
            pltpu.VMEM((128, 1280), bf16),
            pltpu.VMEM((1024, 128), bf16),
            pltpu.VMEM((128, 16, 256), bf16),
            pltpu.VMEM((128, 16, 256), bf16),
            pltpu.VMEM((16, 128), f32),
            pltpu.VMEM((128, 128), f32),
            pltpu.VMEM((16, 8, 128), f32),
            pltpu.VMEM((8, 128), f32),
            pltpu.VMEM((4, 8, 128), f32),
            pltpu.VMEM((8, 128), f32),
            pltpu.VMEM((16, 8, 128), f32),
            pltpu.VMEM((32, 128), f32),
            pltpu.VMEM((64, 128), f32),
            pltpu.VMEM((16, 8, 128), f32),
            pltpu.VMEM((32, 128), f32),
            pltpu.VMEM((4, 32, 128), f32),
            pltpu.VMEM((16, 128), bf16),
            pltpu.VMEM((8, 16, 128), bf16),
            pltpu.VMEM((16, 128), f32),
            pltpu.VMEM((8, 16, 128), f32),
            pltpu.VMEM((3, 4, 128), f32),
            dma((5,)),
            dma,
            dma,
            dma,
            dma((7,)),
            dma((7,)),
        ],
        compiler_params=pltpu.CompilerParams(
            collective_id=0, has_side_effects=True, vmem_limit_bytes=32 * 1024 * 1024
        ),
        name="decode_and_relay",
    )(
        new_hidden,
        norm_gain.reshape(1, 128),
        jnp.asarray(inverse_table()),
        lengths,
        owner_device.reshape(1, 64),
        block_target.reshape(64, 1, 128),
        qkv_weight.reshape(128, 1280),
        out_weight.reshape(1024, 128),
        owned_cache.reshape(128, 16, 256),
    )
    return attended, relaid.reshape(128, 16, 1, 256)


def solution(mesh):
    in_specs = (
        P(None, None, "ctx"),
        P("ctx"),
        P("ctx", "tp", None),
        P("tp", None, "ctx"),
        P("ctx", None, "tp", None),
        P(),
        P(),
        P(),
    )
    out_specs = (P(None, None, "ctx"), P("ctx", None, "tp", None))
    return jax.shard_map(body, mesh=mesh, in_specs=in_specs, out_specs=out_specs, check_vma=False)
```

time: 803 us -> 86.4 us (0.11)
  the two profiles are of different devices: /device:TPU:24 before, /device:TPU:1 now
where the time goes in v1:
time: 86.4 us; the launch traced here: 86.1 us
  Pallas kernels  79.3 us (92%)
  local copies, waits for them, and re-layouts  6.13 us (7%)
    pallas_call x1, Pallas kernels, body(): pl.pallas_call(kernel, out_shape=(jax.ShapeDtypeStruct((3, 4, 128), bf16)...  79.3 us
    unnamed x20, local copies, waits for them, and re-layouts  6.13 us

profile of v1, /device:TPU:1, one launch (start us, length us, event | category | flops | bytes accessed | tf_op | source)
XLA Modules:
  0.0 86.1 jit_solution(558582925402086016)
XLA Ops:
  0.6 0.0 copy-start.4
  0.6 0.0 copy-start.8
  0.7 0.0 copy-start.5
  0.7 0.0 copy-start.6
  0.7 0.0 copy-start.7
  0.7 0.6 copy-done.4
  1.3 0.0 copy-done.8
  1.3 0.0 copy-done.5
  1.3 0.0 copy-done.6
  1.3 0.0 copy-done.7
  1.4 0.0 copy-start
  1.4 1.2 %copy-done = bf16[128,16,1,256]{3,1,2,0:T(8,128)(2,1)S(1)} copy-done((bf16[128,16,1,256]{3,1,2,0:T(8,128)(2,1)S(1)}, bf16[128,16,1,256]{3,1,2,0:T(8,128)(2,1)}, u32[]{:S(2)}) %copy-start) | copy-done | bytes 1048600
  2.6 0.0 copy-start.1
  2.6 1.0 %copy-done.1 = bf16[128,1,1280]{2,0,1:T(8,128)(2,1)S(1)} copy-done((bf16[128,1,1280]{2,0,1:T(8,128)(2,1)S(1)}, bf16[128,1,1280]{2,0,1:T(8,128)(2,1)}, u32[]{:S(2)}) %copy-start.1) | copy-done | bytes 327704
  3.6 0.0 copy-start.2
  3.6 0.9 %copy-done.2 = bf16[1,1024,128]{2,1,0:T(8,128)(2,1)S(1)} copy-done((bf16[1,1024,128]{2,1,0:T(8,128)(2,1)S(1)}, bf16[1,1024,128]{2,1,0:T(8,128)(2,1)}, u32[]{:S(2)}) %copy-start.2) | copy-done | bytes 262168
  4.5 0.0 copy-start.3
  4.5 0.8 copy-done.3
  5.3 79.3 %decode_and_relay.1 = (bf16[3,4,128]{2,1,0:T(4,128)(2,1)S(1)}, bf16[128,16,256]{2,1,0:T(8,128)(2,1)S(1)}) custom-call(bf16[3,4,128]{2,1,0:T(4,128)(2,1)S(1)} %copy-done.4, f32[1,128]{1,0:T(1,128)S(1)} %bitcast.14, f32[1,128]{1,0:T(1,128)S(1)} %copy-done.8, s32[4]{0:T(128)S(1)} %copy-done.6, s32[1,64]{1,0:T(1,128)S(1)} %bitcast.15, ...), custom_call_target="tpu_custom_call" | custom-call | tf_op jit(solution)/shard_map/decode_and_relay/pallas_call | solution.py:378
  84.5 0.6 copy.14
  85.1 1.0 %copy.15 = bf16[128,16,1,256]{3,1,2,0:T(8,128)(2,1)} copy(bf16[128,16,1,256]{3,1,2,0:T(8,128)(2,1)S(1)} %bitcast.10) | data formatting | bytes 2097152
Async XLA Ops:
  0.6 0.7 copy-start.4
  0.6 0.7 copy-start.8
  0.7 0.7 copy-start.5
  0.7 0.7 copy-start.6
  0.7 0.7 copy-start.7
  1.4 1.2 %copy-start = (bf16[128,16,1,256]{3,1,2,0:T(8,128)(2,1)S(1)}, bf16[128,16,1,256]{3,1,2,0:T(8,128)(2,1)}, u32[]{:S(2)}) copy-start(bf16[128,16,1,256]{3,1,2,0:T(8,128)(2,1)} %param.13) | copy-start | bytes 3145732
  2.6 1.0 %copy-start.1 = (bf16[128,1,1280]{2,0,1:T(8,128)(2,1)S(1)}, bf16[128,1,1280]{2,0,1:T(8,128)(2,1)}, u32[]{:S(2)}) copy-start(bf16[128,1,1280]{2,0,1:T(8,128)(2,1)} %param.11) | copy-start | bytes 983044
  3.6 0.9 %copy-start.2 = (bf16[1,1024,128]{2,1,0:T(8,128)(2,1)S(1)}, bf16[1,1024,128]{2,1,0:T(8,128)(2,1)}, u32[]{:S(2)}) copy-start(bf16[1,1024,128]{2,1,0:T(8,128)(2,1)} %param.12) | copy-start | bytes 786436
  4.5 0.8 copy-start.3

commit v2 on v1

--- a/solution.py
+++ b/solution.py
@@ -13,6 +13,7 @@
 ZN, XN, TP = 16, 4, 8
 HEADS = 8
 LOW = -1e30
+VL = 60
 
 
 def remote(src, dst, send, recv, target):
@@ -35,10 +36,10 @@
 
 
 def kernel(
-    hid_ref, gain_ref, inv_ref, len_ref, own_ref, tgt_hbm, wq_hbm, wo_hbm, cache_hbm,
+    len_ref, hid_hbm, gain_hbm, inv_hbm, own_hbm, tgt_hbm, wq_hbm, wo_hbm, cache_hbm,
     att_ref, rel_ref,
-    tgt, slot_v, slot_s, wq, wo, cache, packed,
-    hid32, pbuf, zbuf, xsend, xbuf, asend, gbuf, kvs,
+    hid_ref, gain_ref, inv_ref, own_ref, tgt, slot_v, slot_s, wq, wo, cache, packed,
+    hid32, pbuf, xbuf, zsend, zbuf, asend, gz, xsend, gbuf, kvs,
     bbuf, zb2, x2send, x2buf, ats, agb, osend, tbuf, fs,
     in_sem, own_sem, a2a_send, a2a_recv, chain_send, chain_recv,
 ):
@@ -70,12 +71,22 @@
     cp_wq = pltpu.make_async_copy(wq_hbm, wq, in_sem.at[1])
     cp_cache = pltpu.make_async_copy(cache_hbm, cache, in_sem.at[2])
     cp_wo = pltpu.make_async_copy(wo_hbm, wo, in_sem.at[3])
+    cp_hid = pltpu.make_async_copy(hid_hbm, hid_ref, in_sem.at[5])
+    cp_gain = pltpu.make_async_copy(gain_hbm, gain_ref, in_sem.at[6])
+    cp_inv = pltpu.make_async_copy(inv_hbm, inv_ref, in_sem.at[7])
+    cp_own_dev = pltpu.make_async_copy(own_hbm, own_ref, in_sem.at[8])
     cp_tgt.start()
+    cp_hid.start()
+    cp_gain.start()
     cp_wq.start()
     cp_cache.start()
+    cp_inv.start()
+    cp_own_dev.start()
     cp_wo.start()
 
     hid32[...] = jnp.zeros_like(hid32)
+    cp_hid.wait()
+    cp_gain.wait()
     for step in range(3):
         hid32[4 * step : 4 * step + 4, :] = hid_ref[step].astype(jnp.float32)
     hidden = hid32[...]
@@ -126,10 +137,12 @@
         jnp.where(seq24 == 1, len_ref[1], jnp.where(seq24 == 2, len_ref[2], len_ref[3])),
     )
     position = length24.astype(jnp.float32) + (row_in // 4).astype(jnp.float32)
+    cp_inv.wait()
     angle = position * inv_ref[...]
     cosine = jnp.cos(angle)
     sine = jnp.where(lane24 < 64, -jnp.sin(angle), jnp.sin(angle))
 
+    cp_own_dev.wait()
     own_iota = lax.broadcasted_iota(jnp.int32, (1, 64), 1)
     segment = jnp.sum(jnp.where(own_ref[...] == me, own_iota, 0), axis=1, keepdims=True)
     my_seq = segment // 16
@@ -142,50 +155,73 @@
 
     pl.semaphore_wait(barrier, ZN * XN - 1 + TP - 1)
 
-    def send_blocks(dzs, low, high):
-        def one(dx, carry):
-            for dz in dzs:
-                to = ((z + dz + ZN) % ZN) * XN + (x + dx) % XN
-                remote(
-                    packed.at[pl.ds(2 * to, 2)], rel_ref.at[mine], a2a_send, a2a_recv, {"ctx": to}
-                ).start()
-            return carry
-
-        lax.fori_loop(low, high, one, 0)
+    def send_blocks(dz, dx):
+        to = ((z + dz + ZN) % ZN) * XN + (x + dx) % XN
+        remote(
+            packed.at[pl.ds(2 * to, 2)], rel_ref.at[mine], a2a_send, a2a_recv, {"ctx": to}
+        ).start()
+
+    def bulk(slot):
+        for odd, dx in PLAN[slot]:
+
+            def both_ways(step, carry):
+                dz = 2 * step + 1 if odd else 2 * step
+                send_blocks(dz, dx)
+                send_blocks(-dz, dx)
+                return carry
+
+            if odd:
+                lax.fori_loop(0, 4, both_ways, 0)
+            else:
+                send_blocks(8, dx)
+                lax.fori_loop(1, 4, both_ways, 0)
+                if dx > 0:
+                    send_blocks(0, dx)
+
+    quarter = pl.ds(pl.multiple_of(32 * x, 32), 32)
+    for dx in range(1, XN):
+        to = (x + dx) % XN
+        remote(
+            pbuf.at[pl.ds(pl.multiple_of(32 * to, 32), 32)], xbuf.at[x],
+            chain_send.at[0], chain_recv.at[0], {"ctx": at_x(dx)},
+        ).start()
+    bulk(0)
+    xbuf[x] = pbuf[quarter, :]
+    wait_bytes(xbuf.at[pl.ds(0, XN - 1)], chain_recv.at[0])
+    total = jnp.sum(xbuf[...], axis=0)
+    for c in range(8):
+        zsend[c] = total[4 * c : 4 * c + 4, :]
+    chunk = z % 8
 
     def scatter_a(dz, carry):
         to = (z + dz) % ZN
         remote(
-            pbuf.at[pl.ds(pl.multiple_of(8 * to, 8), 8)], zbuf.at[z],
-            chain_send.at[0], chain_recv.at[0], {"ctx": to * XN + x},
+            zsend.at[to % 8], zbuf.at[z], chain_send.at[1], chain_recv.at[1], {"ctx": to * XN + x}
         ).start()
         return carry
 
     lax.fori_loop(1, ZN, scatter_a, 0)
-    send_blocks(A2A_PLAN[0][0], *A2A_PLAN[0][1])
-    zbuf[z] = pbuf[pl.ds(pl.multiple_of(8 * z, 8), 8), :]
-    wait_bytes(zbuf.at[pl.ds(0, ZN - 1)], chain_recv.at[0])
+    bulk(1)
+    zbuf[z] = zsend[chunk]
+    wait_bytes(zbuf.at[pl.ds(0, ZN - 1)], chain_recv.at[1])
     total = jnp.sum(zbuf[...], axis=0)
-    xsend[...] = total
-    xbuf[x] = total
+    asend[...] = total
+    gz[chunk] = total
+    for dz in (1, -1, 2, -2, 3, -3, 4):
+        remote(
+            asend, gz.at[chunk], chain_send.at[2], chain_recv.at[2], {"ctx": at_z(dz + ZN)}
+        ).start()
+    bulk(2)
+    wait_bytes(gz.at[pl.ds(0, 7)], chain_recv.at[2])
+    for c in range(8):
+        xsend[4 * c : 4 * c + 4, :] = gz[c]
     for dx in range(1, XN):
         remote(
-            xsend, xbuf.at[x], chain_send.at[1], chain_recv.at[1], {"ctx": at_x(dx)}
-        ).start()
-    wait_bytes(xbuf.at[pl.ds(0, XN - 1)], chain_recv.at[1])
-    total = jnp.sum(xbuf[...], axis=0)
-    asend[...] = total
-    gbuf[z] = total
-
-    def gather_a(dz, carry):
-        remote(
-            asend, gbuf.at[z], chain_send.at[2], chain_recv.at[2], {"ctx": at_z(dz)}
-        ).start()
-        return carry
-
-    lax.fori_loop(1, ZN, gather_a, 0)
-    send_blocks(A2A_PLAN[1][0], *A2A_PLAN[1][1])
-    wait_bytes(gbuf.at[pl.ds(0, ZN - 1)], chain_recv.at[2])
+            xsend, gbuf.at[x], chain_send.at[3], chain_recv.at[3], {"ctx": at_x(dx)}
+        ).start()
+    bulk(3)
+    gbuf[x] = xsend[...]
+    wait_bytes(gbuf.at[pl.ds(0, XN - 1)], chain_recv.at[3])
 
     whole = gbuf[...].reshape(128, 128)
     square_sum = jnp.sum(
@@ -203,12 +239,10 @@
     kvs[24:32, :] = jnp.zeros((8, 128), jnp.float32)
     queries = jnp.concatenate(rotated, axis=0).astype(jnp.bfloat16)
 
-    pick_row = lax.broadcasted_iota(jnp.int32, (64, 96), 0)
-    pick_col = lax.broadcasted_iota(jnp.int32, (64, 96), 1)
-    in_tile = pick_row % 8
-    tile_step = jnp.where(in_tile >= 3, in_tile - 3, in_tile)
-    wanted = 12 * (pick_row // 8) + 4 * tile_step + my_seq
-    pick = jnp.where((wanted == pick_col) & (in_tile < 6), 1.0, 0.0).astype(jnp.bfloat16)
+    pick_row = lax.broadcasted_iota(jnp.int32, (32, 96), 0)
+    pick_col = lax.broadcasted_iota(jnp.int32, (32, 96), 1)
+    wanted = 12 * (pick_row // 4) + 4 * (pick_row % 4) + my_seq
+    pick = jnp.where((wanted == pick_col) & (pick_row % 4 < 3), 1.0, 0.0).astype(jnp.bfloat16)
     my_queries = jnp.dot(pick, queries, preferred_element_type=jnp.float32).astype(jnp.bfloat16)
     keys = cache[:, :, 0:128].reshape(2048, 128)
     values = cache[:, :, 128:256].reshape(2048, 128)
@@ -226,26 +260,29 @@
     weights = jnp.where(live, jnp.exp(scores - highest), 0.0)
     weight_sum = jnp.sum(weights, axis=1, keepdims=True)
     weighted = jnp.dot(weights.astype(jnp.bfloat16), values, preferred_element_type=jnp.float32)
-    row64 = lax.broadcasted_iota(jnp.int32, (64, 128), 0) % 8
-    lane64 = lax.broadcasted_iota(jnp.int32, (64, 128), 1)
-    stats = jnp.where(lane64 < 64, highest, weight_sum)
-    bbuf[...] = jnp.where(
-        row64 < 3, weighted, jnp.where(row64 < 6, stats, my_seq.astype(jnp.float32))
-    )
+    row32 = lax.broadcasted_iota(jnp.int32, (32, 128), 0) % 4
+    lane32 = lax.broadcasted_iota(jnp.int32, (32, 128), 1)
+    stats = jnp.where(lane32 < 3, highest, weight_sum)
+    placed = my_seq.astype(jnp.float32)
+    for step in range(3):
+        shifted = pltpu.roll(stats, 3 - step, 0)
+        placed = jnp.where((lane32 == step) | (lane32 == 3 + step), shifted, placed)
+    partial = jnp.where(row32 < 3, weighted, placed)
+    for h in range(HEADS):
+        bbuf[h] = partial[4 * h : 4 * h + 4, :]
 
     head = z % HEADS
 
     def scatter_b(dz, carry):
         to = (z + dz) % ZN
         remote(
-            bbuf.at[pl.ds(pl.multiple_of(8 * (to % HEADS), 8), 8)], zb2.at[z],
-            chain_send.at[3], chain_recv.at[3], {"ctx": to * XN + x},
+            bbuf.at[to % HEADS], zb2.at[z], chain_send.at[4], chain_recv.at[4], {"ctx": to * XN + x}
         ).start()
         return carry
 
     lax.fori_loop(1, ZN, scatter_b, 0)
-    send_blocks(A2A_PLAN[2][0], *A2A_PLAN[2][1])
-    zb2[z] = bbuf[pl.ds(pl.multiple_of(8 * head, 8), 8), :]
+    bulk(4)
+    zb2[z] = bbuf[head]
 
     pick_row = lax.broadcasted_iota(jnp.int32, (16, 96), 0)
     pick_col = lax.broadcasted_iota(jnp.int32, (16, 96), 1)
@@ -269,30 +306,30 @@
     fresh_high = jnp.max(fresh, axis=1, keepdims=True)
     x2send[...] = jnp.where(lax.broadcasted_iota(jnp.int32, (32, 128), 0) < 16, 0.0, 1.0)
 
-    wait_bytes(zb2.at[pl.ds(0, ZN - 1)], chain_recv.at[3])
-    tiles = zb2[...]
-    lane_t = lax.broadcasted_iota(jnp.int32, (16, 8, 128), 2)
-    moved = pltpu.roll(tiles, 5, 1)
-    turned = swap_halves(moved, 2)
-    part_high = jnp.where(lane_t < 64, moved, turned)
-    part_sum = jnp.where(lane_t < 64, turned, moved)
-    part_seq = tiles[:, 6:7, :]
+    wait_bytes(zb2.at[pl.ds(0, ZN - 1)], chain_recv.at[4])
+    stats = zb2[:, 3, :]
+    part_sum = pltpu.roll(stats, 125, 1)
+    part_seq = stats[:, 6:7]
+    lane1 = lax.broadcasted_iota(jnp.int32, (1, 128), 1)
     for seq in range(4):
         member = part_seq == float(seq)
-        high = jnp.max(jnp.where(member, part_high, LOW), axis=0)
-        factor = jnp.where(member, jnp.exp(part_high - high[None]), 0.0)
-        sums = jnp.sum(factor * part_sum, axis=0)
-        accs = jnp.sum(factor * tiles, axis=0)
-        both = jnp.where(lane8 < 64, high, sums)
-        x2send[3 * seq : 3 * seq + 3, :] = accs[0:3, :]
-        x2send[16 + 3 * seq : 16 + 3 * seq + 3, :] = both[0:3, :]
+        high = jnp.max(jnp.where(member, stats, LOW), axis=0, keepdims=True)
+        factor = jnp.where(member, jnp.exp(stats - high), 0.0)
+        sums = jnp.sum(factor * part_sum, axis=0, keepdims=True)
+        for step in range(3):
+            r = 3 * seq + step
+            accs = jnp.sum(factor[:, step : step + 1] * zb2[:, step, :], axis=0, keepdims=True)
+            x2send[r : r + 1, :] = accs
+            x2send[16 + r : 17 + r, :] = jnp.where(
+                lane1 < 64, high[:, step : step + 1], sums[:, step : step + 1]
+            )
     x2buf[x] = x2send[...]
     for dx in range(1, XN):
         remote(
-            x2send, x2buf.at[x], chain_send.at[4], chain_recv.at[4], {"ctx": at_x(dx)}
-        ).start()
-    send_blocks(A2A_PLAN[3][0], *A2A_PLAN[3][1])
-    wait_bytes(x2buf.at[pl.ds(0, XN - 1)], chain_recv.at[4])
+            x2send, x2buf.at[x], chain_send.at[5], chain_recv.at[5], {"ctx": at_x(dx)}
+        ).start()
+    bulk(5)
+    wait_bytes(x2buf.at[pl.ds(0, XN - 1)], chain_recv.at[5])
     accs = x2buf[:, 0:16, :]
     stats = x2buf[:, 16:32, :]
     lane_x = lax.broadcasted_iota(jnp.int32, (4, 16, 128), 2)
@@ -311,11 +348,11 @@
     agb[head] = attention
     for dz in (1, -1, 2, -2, 3, -3, 4):
         remote(
-            ats, agb.at[head], chain_send.at[5], chain_recv.at[5], {"ctx": at_z(dz + ZN)}
-        ).start()
-    send_blocks(A2A_PLAN[4][0], *A2A_PLAN[4][1])
+            ats, agb.at[head], chain_send.at[6], chain_recv.at[6], {"ctx": at_z(dz + ZN)}
+        ).start()
+    bulk(6)
     cp_wo.wait()
-    wait_bytes(agb.at[pl.ds(0, HEADS - 1)], chain_recv.at[5])
+    wait_bytes(agb.at[pl.ds(0, HEADS - 1)], chain_recv.at[6])
 
     out = jnp.zeros((16, 128), jnp.float32)
     for h in range(HEADS):
@@ -326,10 +363,10 @@
     tbuf[mt] = out
     for dt in range(1, TP):
         remote(
-            osend, tbuf.at[mt], chain_send.at[6], chain_recv.at[6], {"tp": (mt + dt) % TP}
-        ).start()
-    send_blocks(A2A_PLAN[5][0], *A2A_PLAN[5][1])
-    wait_bytes(tbuf.at[pl.ds(0, TP - 1)], chain_recv.at[6])
+            osend, tbuf.at[mt], chain_send.at[7], chain_recv.at[7], {"tp": (mt + dt) % TP}
+        ).start()
+    bulk(7)
+    wait_bytes(tbuf.at[pl.ds(0, TP - 1)], chain_recv.at[7])
     out = jnp.sum(tbuf[...], axis=0)
     for step in range(3):
         for seq in range(4):
@@ -337,27 +374,21 @@
             fs[step, seq : seq + 1, :] = out[r : r + 1, :]
     att_ref[...] = fs[...].astype(jnp.bfloat16)
 
-    wait_bytes(pbuf.at[pl.ds(0, 8 * (ZN - 1))], chain_send.at[0])
-    wait_bytes(xbuf.at[pl.ds(0, XN - 1)], chain_send.at[1])
-    wait_bytes(gbuf.at[pl.ds(0, ZN - 1)], chain_send.at[2])
-    wait_bytes(zb2.at[pl.ds(0, ZN - 1)], chain_send.at[3])
-    wait_bytes(x2buf.at[pl.ds(0, XN - 1)], chain_send.at[4])
-    wait_bytes(agb.at[pl.ds(0, HEADS - 1)], chain_send.at[5])
-    wait_bytes(tbuf.at[pl.ds(0, TP - 1)], chain_send.at[6])
+    wait_bytes(xbuf.at[pl.ds(0, XN - 1)], chain_send.at[0])
+    wait_bytes(zbuf.at[pl.ds(0, ZN - 1)], chain_send.at[1])
+    wait_bytes(gz.at[pl.ds(0, 7)], chain_send.at[2])
+    wait_bytes(gbuf.at[pl.ds(0, XN - 1)], chain_send.at[3])
+    wait_bytes(zb2.at[pl.ds(0, ZN - 1)], chain_send.at[4])
+    wait_bytes(x2buf.at[pl.ds(0, XN - 1)], chain_send.at[5])
+    wait_bytes(agb.at[pl.ds(0, HEADS - 1)], chain_send.at[6])
+    wait_bytes(tbuf.at[pl.ds(0, TP - 1)], chain_send.at[7])
     cp_own.wait()
     others = pl.ds(0, 2 * (ZN * XN - 1))
     wait_bytes(packed.at[others], a2a_send)
     wait_bytes(rel_ref.at[others], a2a_recv)
 
 
-A2A_PLAN = (
-    ((1, -1, 7, -7), (0, 4)),
-    ((2, -2, 6, -6), (0, 4)),
-    ((3, -3, 5, -5), (0, 4)),
-    ((4, -4, 8), (0, 4)),
-    ((0,), (1, 4)),
-    ((), (0, 0)),
-)
+PLAN = (((True, 0), ), ((False, 0), ), ((True, 1), ), ((False, 1), ), ((True, 2), (False, 2), ), (), ((True, 3), (False, 3), ), ())
 
 
 def inverse_table():
@@ -373,7 +404,7 @@
     f32, bf16, i32 = jnp.float32, jnp.bfloat16, jnp.int32
     vmem = pl.BlockSpec(memory_space=pltpu.VMEM)
     smem = pl.BlockSpec(memory_space=pltpu.SMEM)
-    hbm = pl.BlockSpec(memory_space=pl.ANY)
+    hbm = pl.BlockSpec(memory_space=pltpu.HBM)
     dma = pltpu.SemaphoreType.DMA
     attended, relaid = pl.pallas_call(
         kernel,
@@ -381,9 +412,13 @@
             jax.ShapeDtypeStruct((3, 4, 128), bf16),
             jax.ShapeDtypeStruct((128, 16, 256), bf16),
         ),
-        in_specs=[vmem, vmem, vmem, smem, vmem, hbm, hbm, hbm, hbm],
+        in_specs=[smem] + [hbm] * 8,
         out_specs=(vmem, hbm),
         scratch_shapes=[
+            pltpu.VMEM((3, 4, 128), bf16),
+            pltpu.VMEM((1, 128), f32),
+            pltpu.VMEM((1, 128), f32),
+            pltpu.VMEM((1, 64), i32),
             pltpu.VMEM((1, 128), i32),
             pltpu.VMEM((64, 128), i32),
             pltpu.SMEM((64, 128), i32),
@@ -393,14 +428,16 @@
             pltpu.VMEM((128, 16, 256), bf16),
             pltpu.VMEM((16, 128), f32),
             pltpu.VMEM((128, 128), f32),
-            pltpu.VMEM((16, 8, 128), f32),
-            pltpu.VMEM((8, 128), f32),
-            pltpu.VMEM((4, 8, 128), f32),
-            pltpu.VMEM((8, 128), f32),
-            pltpu.VMEM((16, 8, 128), f32),
+            pltpu.VMEM((4, 32, 128), f32),
+            pltpu.VMEM((8, 4, 128), f32),
+            pltpu.VMEM((16, 4, 128), f32),
+            pltpu.VMEM((4, 128), f32),
+            pltpu.VMEM((8, 4, 128), f32),
             pltpu.VMEM((32, 128), f32),
-            pltpu.VMEM((64, 128), f32),
-            pltpu.VMEM((16, 8, 128), f32),
+            pltpu.VMEM((4, 32, 128), f32),
+            pltpu.VMEM((32, 128), f32),
+            pltpu.VMEM((8, 4, 128), f32),
+            pltpu.VMEM((16, 4, 128), f32),
             pltpu.VMEM((32, 128), f32),
             pltpu.VMEM((4, 32, 128), f32),
             pltpu.VMEM((16, 128), bf16),
@@ -408,22 +445,22 @@
             pltpu.VMEM((16, 128), f32),
             pltpu.VMEM((8, 16, 128), f32),
             pltpu.VMEM((3, 4, 128), f32),
-            dma((5,)),
+            dma((9,)),
             dma,
             dma,
             dma,
-            dma((7,)),
-            dma((7,)),
+            dma((8,)),
+            dma((8,)),
         ],
         compiler_params=pltpu.CompilerParams(
-            collective_id=0, has_side_effects=True, vmem_limit_bytes=32 * 1024 * 1024
+            collective_id=0, has_side_effects=True, vmem_limit_bytes=VL * 1024 * 1024
         ),
         name="decode_and_relay",
     )(
+        lengths,
         new_hidden,
         norm_gain.reshape(1, 128),
         jnp.asarray(inverse_table()),
-        lengths,
         owner_device.reshape(1, 64),
         block_target.reshape(64, 1, 128),
         qkv_weight.reshape(128, 1280),

time: 86.4 us -> 77.6 us (0.90)
  the two profiles are of different devices: /device:TPU:1 before, /device:TPU:24 now
where the time goes in v2:
time: 77.6 us; the launch traced here: 77.3 us
  Pallas kernels  73.2 us (94%)
  local copies, waits for them, and re-layouts  3.49 us (4%)
    pallas_call x1, Pallas kernels, body(): pl.pallas_call(kernel, out_shape=(jax.ShapeDtypeStruct((3, 4, 128), bf16)...  73.2 us
    unnamed x4, local copies, waits for them, and re-layouts  3.49 us

profile of v2, /device:TPU:24, one launch (start us, length us, event | category | flops | bytes accessed | tf_op | source)
XLA Modules:
  0.0 77.3 jit_solution(9139474911438246299)
XLA Ops:
  0.6 73.2 %decode_and_relay.1 = (bf16[3,4,128]{2,1,0:T(4,128)(2,1)}, bf16[128,16,256]{2,1,0:T(8,128)(2,1)}) custom-call(s32[4]{0:T(128)} %len_ref.1, bf16[3,4,128]{2,1,0:T(4,128)(2,1)} %hid_hbm.1, f32[1,128]{1,0:T(1,128)} %bitcast.14, f32[1,128]{1,0:T(1,128)} %constant.2.clone.inv_hbm, s32[1,64]{1,0:T(1,128)} %bitcast.15, s32[64,1,128]{2,1,0:T(1,128)} %bitcast.13, ...), custom_call_target="tpu_custom_call" | custom-call | tf_op jit(solution)/shard_map/decode_and_relay/pallas_call | solution.py:409
  73.8 0.0 copy-start
  73.8 0.7 copy-done
  74.5 0.6 copy.14
  75.1 2.3 %copy.15 = bf16[128,16,1,256]{3,1,2,0:T(8,128)(2,1)} copy(bf16[128,16,1,256]{3,1,2,0:T(8,128)(2,1)} %bitcast.10) | data formatting | bytes 2097152
Async XLA Ops:
  73.8 0.7 copy-start

commit v3 on v2

--- a/solution.py
+++ b/solution.py
@@ -39,7 +39,7 @@
     len_ref, hid_hbm, gain_hbm, inv_hbm, own_hbm, tgt_hbm, wq_hbm, wo_hbm, cache_hbm,
     att_ref, rel_ref,
     hid_ref, gain_ref, inv_ref, own_ref, tgt, slot_v, slot_s, wq, wo, cache, packed,
-    hid32, pbuf, xbuf, zsend, zbuf, asend, gz, xsend, gbuf, kvs,
+    hid32, pbuf, xbuf, zsend, zbuf, asend, gbuf, kvs,
     bbuf, zb2, x2send, x2buf, ats, agb, osend, tbuf, fs,
     in_sem, own_sem, a2a_send, a2a_recv, chain_send, chain_recv,
 ):
@@ -56,15 +56,21 @@
 
     barrier = pltpu.get_barrier_semaphore()
 
+    def greet(offset):
+        to = (me + ZN * XN + offset) % (ZN * XN)
+        pl.semaphore_signal(barrier, inc=1, device_id={"ctx": to}, device_id_type=MESH)
+
     def greet_ctx(k, carry):
-        pl.semaphore_signal(barrier, inc=1, device_id={"ctx": (me + k) % (ZN * XN)}, device_id_type=MESH)
+        greet(32 + k)
+        greet(32 - k)
         return carry
 
     def greet_tp(k, carry):
         pl.semaphore_signal(barrier, inc=1, device_id={"tp": (mt + k) % TP}, device_id_type=MESH)
         return carry
 
-    lax.fori_loop(1, ZN * XN, greet_ctx, 0)
+    greet(32)
+    lax.fori_loop(1, 32, greet_ctx, 0)
     lax.fori_loop(1, TP, greet_tp, 0)
 
     cp_tgt = pltpu.make_async_copy(tgt_hbm.at[me], tgt, in_sem.at[0])
@@ -178,8 +184,17 @@
                 if dx > 0:
                     send_blocks(0, dx)
 
+    def far_first(send):
+        def both_ways(step, carry):
+            send(ZN // 2 + step)
+            send(ZN // 2 - step)
+            return carry
+
+        send(ZN // 2)
+        lax.fori_loop(1, ZN // 2, both_ways, 0)
+
     quarter = pl.ds(pl.multiple_of(32 * x, 32), 32)
-    for dx in range(1, XN):
+    for dx in (2, 1, 3):
         to = (x + dx) % XN
         remote(
             pbuf.at[pl.ds(pl.multiple_of(32 * to, 32), 32)], xbuf.at[x],
@@ -189,39 +204,30 @@
     xbuf[x] = pbuf[quarter, :]
     wait_bytes(xbuf.at[pl.ds(0, XN - 1)], chain_recv.at[0])
     total = jnp.sum(xbuf[...], axis=0)
-    for c in range(8):
-        zsend[c] = total[4 * c : 4 * c + 4, :]
-    chunk = z % 8
-
-    def scatter_a(dz, carry):
+    zsend[...] = total.reshape(4, 8, 128)
+    chunk = z % 4
+
+    def scatter_a(dz):
         to = (z + dz) % ZN
         remote(
-            zsend.at[to % 8], zbuf.at[z], chain_send.at[1], chain_recv.at[1], {"ctx": to * XN + x}
-        ).start()
-        return carry
-
-    lax.fori_loop(1, ZN, scatter_a, 0)
+            zsend.at[to % 4], zbuf.at[z], chain_send.at[1], chain_recv.at[1], {"ctx": to * XN + x}
+        ).start()
+
+    far_first(scatter_a)
     bulk(1)
     zbuf[z] = zsend[chunk]
     wait_bytes(zbuf.at[pl.ds(0, ZN - 1)], chain_recv.at[1])
     total = jnp.sum(zbuf[...], axis=0)
     asend[...] = total
-    gz[chunk] = total
-    for dz in (1, -1, 2, -2, 3, -3, 4):
-        remote(
-            asend, gz.at[chunk], chain_send.at[2], chain_recv.at[2], {"ctx": at_z(dz + ZN)}
+    gbuf[x, chunk] = total
+    for dz, dx in ((2, 2), (2, 1), (2, 3), (1, 2), (-1, 2), (1, 1), (-1, 1), (1, 3), (-1, 3),
+                   (2, 0), (0, 2), (1, 0), (-1, 0), (0, 1), (0, 3)):
+        to = ((z + dz + ZN) % ZN) * XN + (x + dx) % XN
+        remote(
+            asend, gbuf.at[x, chunk], chain_send.at[2], chain_recv.at[2], {"ctx": to}
         ).start()
     bulk(2)
-    wait_bytes(gz.at[pl.ds(0, 7)], chain_recv.at[2])
-    for c in range(8):
-        xsend[4 * c : 4 * c + 4, :] = gz[c]
-    for dx in range(1, XN):
-        remote(
-            xsend, gbuf.at[x], chain_send.at[3], chain_recv.at[3], {"ctx": at_x(dx)}
-        ).start()
-    bulk(3)
-    gbuf[x] = xsend[...]
-    wait_bytes(gbuf.at[pl.ds(0, XN - 1)], chain_recv.at[3])
+    wait_bytes(zbuf.at[pl.ds(0, 15)], chain_recv.at[2])
 
     whole = gbuf[...].reshape(128, 128)
     square_sum = jnp.sum(
@@ -273,15 +279,14 @@
 
     head = z % HEADS
 
-    def scatter_b(dz, carry):
+    def scatter_b(dz):
         to = (z + dz) % ZN
         remote(
-            bbuf.at[to % HEADS], zb2.at[z], chain_send.at[4], chain_recv.at[4], {"ctx": to * XN + x}
-        ).start()
-        return carry
-
-    lax.fori_loop(1, ZN, scatter_b, 0)
-    bulk(4)
+            bbuf.at[to % HEADS], zb2.at[z], chain_send.at[3], chain_recv.at[3], {"ctx": to * XN + x}
+        ).start()
+
+    far_first(scatter_b)
+    bulk(3)
     zb2[z] = bbuf[head]
 
     pick_row = lax.broadcasted_iota(jnp.int32, (16, 96), 0)
@@ -306,7 +311,7 @@
     fresh_high = jnp.max(fresh, axis=1, keepdims=True)
     x2send[...] = jnp.where(lax.broadcasted_iota(jnp.int32, (32, 128), 0) < 16, 0.0, 1.0)
 
-    wait_bytes(zb2.at[pl.ds(0, ZN - 1)], chain_recv.at[4])
+    wait_bytes(zb2.at[pl.ds(0, ZN - 1)], chain_recv.at[3])
     stats = zb2[:, 3, :]
     part_sum = pltpu.roll(stats, 125, 1)
     part_seq = stats[:, 6:7]
@@ -324,12 +329,12 @@
                 lane1 < 64, high[:, step : step + 1], sums[:, step : step + 1]
             )
     x2buf[x] = x2send[...]
-    for dx in range(1, XN):
-        remote(
-            x2send, x2buf.at[x], chain_send.at[5], chain_recv.at[5], {"ctx": at_x(dx)}
-        ).start()
-    bulk(5)
-    wait_bytes(x2buf.at[pl.ds(0, XN - 1)], chain_recv.at[5])
+    for dx in (2, 1, 3):
+        remote(
+            x2send, x2buf.at[x], chain_send.at[4], chain_recv.at[4], {"ctx": at_x(dx)}
+        ).start()
+    bulk(4)
+    wait_bytes(x2buf.at[pl.ds(0, XN - 1)], chain_recv.at[4])
     accs = x2buf[:, 0:16, :]
     stats = x2buf[:, 16:32, :]
     lane_x = lax.broadcasted_iota(jnp.int32, (4, 16, 128), 2)
@@ -346,13 +351,13 @@
     attention = (mixed / sums).astype(jnp.bfloat16)
     ats[...] = attention
     agb[head] = attention
-    for dz in (1, -1, 2, -2, 3, -3, 4):
-        remote(
-            ats, agb.at[head], chain_send.at[6], chain_recv.at[6], {"ctx": at_z(dz + ZN)}
-        ).start()
-    bulk(6)
+    for dz in (4, 3, -3, 2, -2, 1, -1):
+        remote(
+            ats, agb.at[head], chain_send.at[5], chain_recv.at[5], {"ctx": at_z(dz + ZN)}
+        ).start()
+    bulk(5)
     cp_wo.wait()
-    wait_bytes(agb.at[pl.ds(0, HEADS - 1)], chain_recv.at[6])
+    wait_bytes(agb.at[pl.ds(0, HEADS - 1)], chain_recv.at[5])
 
     out = jnp.zeros((16, 128), jnp.float32)
     for h in range(HEADS):
@@ -361,12 +366,12 @@
         )
     osend[...] = out
     tbuf[mt] = out
-    for dt in range(1, TP):
-        remote(
-            osend, tbuf.at[mt], chain_send.at[7], chain_recv.at[7], {"tp": (mt + dt) % TP}
-        ).start()
-    bulk(7)
-    wait_bytes(tbuf.at[pl.ds(0, TP - 1)], chain_recv.at[7])
+    for dt in (4, 5, 3, 2, 6, 1, 7):
+        remote(
+            osend, tbuf.at[mt], chain_send.at[6], chain_recv.at[6], {"tp": (mt + dt) % TP}
+        ).start()
+    bulk(6)
+    wait_bytes(tbuf.at[pl.ds(0, TP - 1)], chain_recv.at[6])
     out = jnp.sum(tbuf[...], axis=0)
     for step in range(3):
         for seq in range(4):
@@ -376,19 +381,18 @@
 
     wait_bytes(xbuf.at[pl.ds(0, XN - 1)], chain_send.at[0])
     wait_bytes(zbuf.at[pl.ds(0, ZN - 1)], chain_send.at[1])
-    wait_bytes(gz.at[pl.ds(0, 7)], chain_send.at[2])
-    wait_bytes(gbuf.at[pl.ds(0, XN - 1)], chain_send.at[3])
-    wait_bytes(zb2.at[pl.ds(0, ZN - 1)], chain_send.at[4])
-    wait_bytes(x2buf.at[pl.ds(0, XN - 1)], chain_send.at[5])
-    wait_bytes(agb.at[pl.ds(0, HEADS - 1)], chain_send.at[6])
-    wait_bytes(tbuf.at[pl.ds(0, TP - 1)], chain_send.at[7])
+    wait_bytes(zbuf.at[pl.ds(0, 15)], chain_send.at[2])
+    wait_bytes(zb2.at[pl.ds(0, ZN - 1)], chain_send.at[3])
+    wait_bytes(x2buf.at[pl.ds(0, XN - 1)], chain_send.at[4])
+    wait_bytes(agb.at[pl.ds(0, HEADS - 1)], chain_send.at[5])
+    wait_bytes(tbuf.at[pl.ds(0, TP - 1)], chain_send.at[6])
     cp_own.wait()
     others = pl.ds(0, 2 * (ZN * XN - 1))
     wait_bytes(packed.at[others], a2a_send)
     wait_bytes(rel_ref.at[others], a2a_recv)
 
 
-PLAN = (((True, 0), ), ((False, 0), ), ((True, 1), ), ((False, 1), ), ((True, 2), (False, 2), ), (), ((True, 3), (False, 3), ), ())
+PLAN = (((True, 0), ), ((False, 0), ), ((True, 1), ), ((False, 1), (True, 2), ), ((False, 2), ), ((True, 3), (False, 3), ), ())
 
 
 def inverse_table():
@@ -409,11 +413,11 @@
     attended, relaid = pl.pallas_call(
         kernel,
         out_shape=(
-            jax.ShapeDtypeStruct((3, 4, 128), bf16),
-            jax.ShapeDtypeStruct((128, 16, 256), bf16),
+            pltpu.VMEM((3, 4, 128), bf16),
+            pltpu.VMEM((128, 16, 256), bf16),
         ),
         in_specs=[smem] + [hbm] * 8,
-        out_specs=(vmem, hbm),
+        out_specs=(vmem, vmem),
         scratch_shapes=[
             pltpu.VMEM((3, 4, 128), bf16),
             pltpu.VMEM((1, 128), f32),
@@ -429,12 +433,10 @@
             pltpu.VMEM((16, 128), f32),
             pltpu.VMEM((128, 128), f32),
             pltpu.VMEM((4, 32, 128), f32),
-            pltpu.VMEM((8, 4, 128), f32),
-            pltpu.VMEM((16, 4, 128), f32),
-            pltpu.VMEM((4, 128), f32),
-            pltpu.VMEM((8, 4, 128), f32),
-            pltpu.VMEM((32, 128), f32),
-            pltpu.VMEM((4, 32, 128), f32),
+            pltpu.VMEM((4, 8, 128), f32),
+            pltpu.VMEM((16, 8, 128), f32),
+            pltpu.VMEM((8, 128), f32),
+            pltpu.VMEM((4, 4, 8, 128), f32),
             pltpu.VMEM((32, 128), f32),
             pltpu.VMEM((8, 4, 128), f32),
             pltpu.VMEM((16, 4, 128), f32),
@@ -449,8 +451,8 @@
             dma,
             dma,
             dma,
-            dma((8,)),
-            dma((8,)),
+            dma((7,)),
+            dma((7,)),
         ],
         compiler_params=pltpu.CompilerParams(
             collective_id=0, has_side_effects=True, vmem_limit_bytes=VL * 1024 * 1024

time: 77.6 us -> 73.1 us (0.942)
  Pallas kernels: 73.2 us -> 70 us
  local copies, waits for them, and re-layouts: 3.49 us -> 1.55 us
    pallas_call x1, Pallas kernels: 73.2 us -> 70 us  [body(): pl.pallas_call(kernel, out_shape=(pltpu.VMEM((3, 4, 128), bf16), pltpu.VM...]
    unnamed x4 -> x2, local copies, waits for them, and re-layouts: 3.49 us -> 1.55 us
where the time goes in v3:
time: 73.1 us; the launch traced here: 72.2 us
  Pallas kernels  70 us (96%)
  local copies, waits for them, and re-layouts  1.55 us (2%)
    pallas_call x1, Pallas kernels, body(): pl.pallas_call(kernel, out_shape=(pltpu.VMEM((3, 4, 128), bf16), pltpu.VM...  70 us
    unnamed x2, local copies, waits for them, and re-layouts  1.55 us

profile of v3, /device:TPU:24, one launch (start us, length us, event | category | flops | bytes accessed | tf_op | source)
XLA Modules:
  0.0 72.2 jit_solution(13599227569306099881)
XLA Ops:
  0.6 70.0 %decode_and_relay.1 = (bf16[3,4,128]{2,1,0:T(4,128)(2,1)S(1)}, bf16[128,16,256]{2,1,0:T(8,128)(2,1)S(1)}) custom-call(s32[4]{0:T(128)} %len_ref.1, bf16[3,4,128]{2,1,0:T(4,128)(2,1)} %hid_hbm.1, f32[1,128]{1,0:T(1,128)} %bitcast.14, f32[1,128]{1,0:T(1,128)} %constant.2.clone.inv_hbm, s32[1,64]{1,0:T(1,128)} %bitcast.15, s32[64,1,128]{2,1,0:T(1,128)} %bitcast.13, ...), custom_call_target="tpu_custom_call" | custom-call | tf_op jit(solution)/shard_map/decode_and_relay/pallas_call | solution.py:413
  70.7 0.6 copy.14
  71.3 1.0 %copy.15 = bf16[128,16,1,256]{3,1,2,0:T(8,128)(2,1)} copy(bf16[128,16,1,256]{3,1,2,0:T(8,128)(2,1)S(1)} %bitcast.9) | data formatting | bytes 2097152

commit v4 on v3

--- a/solution.py
+++ b/solution.py
@@ -41,7 +41,7 @@
     hid_ref, gain_ref, inv_ref, own_ref, tgt, slot_v, slot_s, wq, wo, cache, packed,
     hid32, pbuf, xbuf, zsend, zbuf, asend, gbuf, kvs,
     bbuf, zb2, x2send, x2buf, ats, agb, osend, tbuf, fs,
-    in_sem, own_sem, a2a_send, a2a_recv, chain_send, chain_recv,
+    in_sem, own_sem, a2a_send, a2a_recv, chain_send, chain_recv, ready,
 ):
     me = lax.axis_index("ctx")
     mt = lax.axis_index("tp")
@@ -56,21 +56,23 @@
 
     barrier = pltpu.get_barrier_semaphore()
 
-    def greet(offset):
-        to = (me + ZN * XN + offset) % (ZN * XN)
+    def greet(dz, dx):
+        to = ((z + dz + ZN) % ZN) * XN + (x + dx) % XN
         pl.semaphore_signal(barrier, inc=1, device_id={"ctx": to}, device_id_type=MESH)
 
-    def greet_ctx(k, carry):
-        greet(32 + k)
-        greet(32 - k)
+    def greet_both(step, carry):
+        for dx in range(XN):
+            greet(4 - step, dx)
+            greet(step - 4, dx)
         return carry
 
     def greet_tp(k, carry):
         pl.semaphore_signal(barrier, inc=1, device_id={"tp": (mt + k) % TP}, device_id_type=MESH)
         return carry
 
-    greet(32)
-    lax.fori_loop(1, 32, greet_ctx, 0)
+    lax.fori_loop(0, 4, greet_both, 0)
+    for dx in range(1, XN):
+        greet(0, dx)
     lax.fori_loop(1, TP, greet_tp, 0)
 
     cp_tgt = pltpu.make_async_copy(tgt_hbm.at[me], tgt, in_sem.at[0])
@@ -120,6 +122,43 @@
     slot_v[...] = jnp.where(b_iota == 0, first, last)
     cp_slot = pltpu.make_async_copy(slot_v, slot_s, in_sem.at[4])
     cp_slot.start()
+    def send_blocks(dz, dx):
+        to = ((z + dz + ZN) % ZN) * XN + (x + dx) % XN
+        remote(
+            packed.at[pl.ds(2 * to, 2)], rel_ref.at[mine], a2a_send, a2a_recv, {"ctx": to}
+        ).start()
+
+    def bulk(slot):
+        for shifts, low, high in PLAN[slot]:
+
+            def one(dx, carry):
+                for dz in shifts:
+                    send_blocks(dz, dx)
+                return carry
+
+            lax.fori_loop(low, high, one, 0)
+
+    def far_first(send):
+        def both_ways(step, carry):
+            send(ZN // 2 + step)
+            send(ZN // 2 - step)
+            return carry
+
+        send(ZN // 2)
+        lax.fori_loop(1, ZN // 2, both_ways, 0)
+
+    pl.semaphore_wait(barrier, 9 * XN - 1 + TP - 1)
+    for dz in (4, -4):
+        pl.semaphore_signal(ready, inc=1, device_id={"ctx": at_z(dz + ZN)}, device_id_type=MESH)
+
+    quarter = pl.ds(pl.multiple_of(32 * x, 32), 32)
+    for dx in (2, 1, 3):
+        to = (x + dx) % XN
+        remote(
+            pbuf.at[pl.ds(pl.multiple_of(32 * to, 32), 32)], xbuf.at[x],
+            chain_send.at[0], chain_recv.at[0], {"ctx": at_x(dx)},
+        ).start()
+
     cp_slot.wait()
     cp_cache.wait()
 
@@ -132,6 +171,23 @@
     mine = pl.ds(2 * me, 2)
     cp_own = pltpu.make_async_copy(packed.at[mine], rel_ref.at[mine], own_sem)
     cp_own.start()
+
+    bulk(0)
+    xbuf[x] = pbuf[quarter, :]
+    wait_bytes(xbuf.at[pl.ds(0, XN - 1)], chain_recv.at[0])
+    total = jnp.sum(xbuf[...], axis=0)
+    pl.semaphore_wait(ready, 2)
+    zsend[...] = total.reshape(4, 8, 128)
+    chunk = z % 4
+
+    def scatter_a(dz):
+        to = (z + dz) % ZN
+        remote(
+            zsend.at[to % 4], zbuf.at[z], chain_send.at[1], chain_recv.at[1], {"ctx": to * XN + x}
+        ).start()
+
+    far_first(scatter_a)
+    bulk(1)
 
     row24 = lax.broadcasted_iota(jnp.int32, (24, 128), 0)
     lane24 = lax.broadcasted_iota(jnp.int32, (24, 128), 1)
@@ -159,62 +215,6 @@
         jnp.where(my_seq == 1, len_ref[1], jnp.where(my_seq == 2, len_ref[2], len_ref[3])),
     )
 
-    pl.semaphore_wait(barrier, ZN * XN - 1 + TP - 1)
-
-    def send_blocks(dz, dx):
-        to = ((z + dz + ZN) % ZN) * XN + (x + dx) % XN
-        remote(
-            packed.at[pl.ds(2 * to, 2)], rel_ref.at[mine], a2a_send, a2a_recv, {"ctx": to}
-        ).start()
-
-    def bulk(slot):
-        for odd, dx in PLAN[slot]:
-
-            def both_ways(step, carry):
-                dz = 2 * step + 1 if odd else 2 * step
-                send_blocks(dz, dx)
-                send_blocks(-dz, dx)
-                return carry
-
-            if odd:
-                lax.fori_loop(0, 4, both_ways, 0)
-            else:
-                send_blocks(8, dx)
-                lax.fori_loop(1, 4, both_ways, 0)
-                if dx > 0:
-                    send_blocks(0, dx)
-
-    def far_first(send):
-        def both_ways(step, carry):
-            send(ZN // 2 + step)
-            send(ZN // 2 - step)
-            return carry
-
-        send(ZN // 2)
-        lax.fori_loop(1, ZN // 2, both_ways, 0)
-
-    quarter = pl.ds(pl.multiple_of(32 * x, 32), 32)
-    for dx in (2, 1, 3):
-        to = (x + dx) % XN
-        remote(
-            pbuf.at[pl.ds(pl.multiple_of(32 * to, 32), 32)], xbuf.at[x],
-            chain_send.at[0], chain_recv.at[0], {"ctx": at_x(dx)},
-        ).start()
-    bulk(0)
-    xbuf[x] = pbuf[quarter, :]
-    wait_bytes(xbuf.at[pl.ds(0, XN - 1)], chain_recv.at[0])
-    total = jnp.sum(xbuf[...], axis=0)
-    zsend[...] = total.reshape(4, 8, 128)
-    chunk = z % 4
-
-    def scatter_a(dz):
-        to = (z + dz) % ZN
-        remote(
-            zsend.at[to % 4], zbuf.at[z], chain_send.at[1], chain_recv.at[1], {"ctx": to * XN + x}
-        ).start()
-
-    far_first(scatter_a)
-    bulk(1)
     zbuf[z] = zsend[chunk]
     wait_bytes(zbuf.at[pl.ds(0, ZN - 1)], chain_recv.at[1])
     total = jnp.sum(zbuf[...], axis=0)
@@ -392,7 +392,8 @@
     wait_bytes(rel_ref.at[others], a2a_recv)
 
 
-PLAN = (((True, 0), ), ((False, 0), ), ((True, 1), ), ((False, 1), (True, 2), ), ((False, 2), ), ((True, 3), (False, 3), ), ())
+NEAR = (((1, -1, 2, -2), 0, 4), ((0,), 1, 4))
+PLAN = (NEAR, (((8,), 0, 4), ((7, -7), 0, 2)), (((7, -7), 2, 4),), (((6, -6), 0, 4), ((5, -5), 0, 2)), (), (((5, -5), 2, 4), ((4, -4), 0, 4)), (((3, -3), 0, 4),))
 
 
 def inverse_table():
@@ -453,6 +454,7 @@
             dma,
             dma((7,)),
             dma((7,)),
+            pltpu.SemaphoreType.REGULAR,
         ],
         compiler_params=pltpu.CompilerParams(
             collective_id=0, has_side_effects=True, vmem_limit_bytes=VL * 1024 * 1024

time: 73.1 us -> 73 us (level); the launches traced: 72.2 us -> 72.9 us
  no operation moved by 1% of the time
where the time goes in v4:
time: 73 us; the launch traced here: 72.9 us
  Pallas kernels  70.7 us (97%)
  local copies, waits for them, and re-layouts  1.55 us (2%)
    pallas_call x1, Pallas kernels, body(): pl.pallas_call(kernel, out_shape=(pltpu.VMEM((3, 4, 128), bf16), pltpu.VM...  70.7 us
    unnamed x2, local copies, waits for them, and re-layouts  1.55 us

profile of v4, /device:TPU:24, one launch (start us, length us, event | category | flops | bytes accessed | tf_op | source)
XLA Modules:
  0.0 72.9 jit_solution(647406129999990988)
XLA Ops:
  0.6 70.7 %decode_and_relay.1 = (bf16[3,4,128]{2,1,0:T(4,128)(2,1)S(1)}, bf16[128,16,256]{2,1,0:T(8,128)(2,1)S(1)}) custom-call(s32[4]{0:T(128)} %len_ref.1, bf16[3,4,128]{2,1,0:T(4,128)(2,1)} %hid_hbm.1, f32[1,128]{1,0:T(1,128)} %bitcast.14, f32[1,128]{1,0:T(1,128)} %constant.2.clone.inv_hbm, s32[1,64]{1,0:T(1,128)} %bitcast.15, s32[64,1,128]{2,1,0:T(1,128)} %bitcast.13, ...), custom_call_target="tpu_custom_call" | custom-call | tf_op jit(solution)/shard_map/decode_and_relay/pallas_call | solution.py:414
  71.3 0.6 copy.14
  71.9 1.0 %copy.15 = bf16[128,16,1,256]{3,1,2,0:T(8,128)(2,1)} copy(bf16[128,16,1,256]{3,1,2,0:T(8,128)(2,1)S(1)} %bitcast.9) | data formatting | bytes 2097152

commit v5 on v4

--- a/solution.py
+++ b/solution.py
@@ -147,18 +147,6 @@
         send(ZN // 2)
         lax.fori_loop(1, ZN // 2, both_ways, 0)
 
-    pl.semaphore_wait(barrier, 9 * XN - 1 + TP - 1)
-    for dz in (4, -4):
-        pl.semaphore_signal(ready, inc=1, device_id={"ctx": at_z(dz + ZN)}, device_id_type=MESH)
-
-    quarter = pl.ds(pl.multiple_of(32 * x, 32), 32)
-    for dx in (2, 1, 3):
-        to = (x + dx) % XN
-        remote(
-            pbuf.at[pl.ds(pl.multiple_of(32 * to, 32), 32)], xbuf.at[x],
-            chain_send.at[0], chain_recv.at[0], {"ctx": at_x(dx)},
-        ).start()
-
     cp_slot.wait()
     cp_cache.wait()
 
@@ -171,6 +159,18 @@
     mine = pl.ds(2 * me, 2)
     cp_own = pltpu.make_async_copy(packed.at[mine], rel_ref.at[mine], own_sem)
     cp_own.start()
+
+    pl.semaphore_wait(barrier, 9 * XN - 1 + TP - 1)
+    for dz in (4, -4):
+        pl.semaphore_signal(ready, inc=1, device_id={"ctx": at_z(dz + ZN)}, device_id_type=MESH)
+
+    quarter = pl.ds(pl.multiple_of(32 * x, 32), 32)
+    for dx in (2, 1, 3):
+        to = (x + dx) % XN
+        remote(
+            pbuf.at[pl.ds(pl.multiple_of(32 * to, 32), 32)], xbuf.at[x],
+            chain_send.at[0], chain_recv.at[0], {"ctx": at_x(dx)},
+        ).start()
 
     bulk(0)
     xbuf[x] = pbuf[quarter, :]
@@ -393,7 +393,7 @@
 
 
 NEAR = (((1, -1, 2, -2), 0, 4), ((0,), 1, 4))
-PLAN = (NEAR, (((8,), 0, 4), ((7, -7), 0, 2)), (((7, -7), 2, 4),), (((6, -6), 0, 4), ((5, -5), 0, 2)), (), (((5, -5), 2, 4), ((4, -4), 0, 4)), (((3, -3), 0, 4),))
+PLAN = (NEAR, (((8,), 0, 4), ((7, -7), 0, 2)), (((7, -7), 2, 4),), (((6, -6), 0, 4), ((5, -5), 0, 4)), (), (((4, -4), 0, 4), ((3, -3), 0, 4)), ())
 
 
 def inverse_table():

time: 73 us -> 71.7 us (0.982); the launches traced: 72.9 us -> 70.7 us
  Pallas kernels: 70.7 us -> 68.6 us
    pallas_call x1, Pallas kernels: 70.7 us -> 68.6 us  [body(): pl.pallas_call(kernel, out_shape=(pltpu.VMEM((3, 4, 128), bf16), pltpu.VM...]
where the time goes in v5:
time: 71.7 us; the launch traced here: 70.7 us
  Pallas kernels  68.6 us (96%)
  local copies, waits for them, and re-layouts  1.55 us (2%)
    pallas_call x1, Pallas kernels, body(): pl.pallas_call(kernel, out_shape=(pltpu.VMEM((3, 4, 128), bf16), pltpu.VM...  68.6 us
    unnamed x2, local copies, waits for them, and re-layouts  1.55 us

profile of v5, /device:TPU:24, one launch (start us, length us, event | category | flops | bytes accessed | tf_op | source)
XLA Modules:
  0.0 70.7 jit_solution(2246419604675117485)
XLA Ops:
  0.6 68.6 %decode_and_relay.1 = (bf16[3,4,128]{2,1,0:T(4,128)(2,1)S(1)}, bf16[128,16,256]{2,1,0:T(8,128)(2,1)S(1)}) custom-call(s32[4]{0:T(128)} %len_ref.1, bf16[3,4,128]{2,1,0:T(4,128)(2,1)} %hid_hbm.1, f32[1,128]{1,0:T(1,128)} %bitcast.14, f32[1,128]{1,0:T(1,128)} %constant.2.clone.inv_hbm, s32[1,64]{1,0:T(1,128)} %bitcast.15, s32[64,1,128]{2,1,0:T(1,128)} %bitcast.13, ...), custom_call_target="tpu_custom_call" | custom-call | tf_op jit(solution)/shard_map/decode_and_relay/pallas_call | solution.py:414
  69.2 0.6 copy.14
  69.8 1.0 %copy.15 = bf16[128,16,1,256]{3,1,2,0:T(8,128)(2,1)} copy(bf16[128,16,1,256]{3,1,2,0:T(8,128)(2,1)S(1)} %bitcast.9) | data formatting | bytes 2097152

commit v6 on v5

--- a/solution.py
+++ b/solution.py
@@ -53,27 +53,6 @@
 
     def at_x(dx):
         return z * XN + (x + dx) % XN
-
-    barrier = pltpu.get_barrier_semaphore()
-
-    def greet(dz, dx):
-        to = ((z + dz + ZN) % ZN) * XN + (x + dx) % XN
-        pl.semaphore_signal(barrier, inc=1, device_id={"ctx": to}, device_id_type=MESH)
-
-    def greet_both(step, carry):
-        for dx in range(XN):
-            greet(4 - step, dx)
-            greet(step - 4, dx)
-        return carry
-
-    def greet_tp(k, carry):
-        pl.semaphore_signal(barrier, inc=1, device_id={"tp": (mt + k) % TP}, device_id_type=MESH)
-        return carry
-
-    lax.fori_loop(0, 4, greet_both, 0)
-    for dx in range(1, XN):
-        greet(0, dx)
-    lax.fori_loop(1, TP, greet_tp, 0)
 
     cp_tgt = pltpu.make_async_copy(tgt_hbm.at[me], tgt, in_sem.at[0])
     cp_wq = pltpu.make_async_copy(wq_hbm, wq, in_sem.at[1])
@@ -91,6 +70,62 @@
     cp_inv.start()
     cp_own_dev.start()
     cp_wo.start()
+
+    barrier = pltpu.get_barrier_semaphore()
+
+    def greet(dz, dx):
+        to = ((z + dz + ZN) % ZN) * XN + (x + dx) % XN
+        pl.semaphore_signal(barrier, inc=1, device_id={"ctx": to}, device_id_type=MESH)
+
+    def greet_both(step, carry):
+        for dx in range(XN):
+            greet(4 - step, dx)
+            greet(step - 4, dx)
+        return carry
+
+    def greet_tp(k, carry):
+        pl.semaphore_signal(barrier, inc=1, device_id={"tp": (mt + k) % TP}, device_id_type=MESH)
+        return carry
+
+    lax.fori_loop(0, 4, greet_both, 0)
+    for dx in range(1, XN):
+        greet(0, dx)
+    lax.fori_loop(1, TP, greet_tp, 0)
+
+    cp_tgt.wait()
+    t_iota = lax.broadcasted_iota(jnp.int32, (64, 128), 0)
+    b_iota = lax.broadcasted_iota(jnp.int32, (64, 128), 1)
+    match = tgt[...] == t_iota
+    first = jnp.min(jnp.where(match, b_iota, 127), axis=1, keepdims=True)
+    last = jnp.max(jnp.where(match, b_iota, 0), axis=1, keepdims=True)
+    slot_v[...] = jnp.where(b_iota == 0, first, last)
+    cp_slot = pltpu.make_async_copy(slot_v, slot_s, in_sem.at[4])
+    cp_slot.start()
+    def send_blocks(dz, dx):
+        to = ((z + dz + ZN) % ZN) * XN + (x + dx) % XN
+        remote(
+            packed.at[pl.ds(2 * to, 2)], rel_ref.at[mine], a2a_send, a2a_recv, {"ctx": to}
+        ).start()
+
+    def bulk(slot):
+        for shifts, low, high in PLAN[slot]:
+
+            def one(dx, carry):
+                for dz in shifts:
+                    send_blocks(dz, dx)
+                return carry
+
+            lax.fori_loop(low, high, one, 0)
+
+    def far_first(send):
+        def both_ways(step, carry):
+            send(ZN // 2 + step)
+            send(ZN // 2 - step)
+            return carry
+
+        send(ZN // 2)
+        lax.fori_loop(1, ZN // 2, both_ways, 0)
+
 
     hid32[...] = jnp.zeros_like(hid32)
     cp_hid.wait()
@@ -112,40 +147,6 @@
             scaled, wq[:, 128 * head : 128 * head + 128], preferred_element_type=jnp.float32
         )
         pbuf[12 * head : 12 * head + 12, :] = part[0:12, :]
-
-    cp_tgt.wait()
-    t_iota = lax.broadcasted_iota(jnp.int32, (64, 128), 0)
-    b_iota = lax.broadcasted_iota(jnp.int32, (64, 128), 1)
-    match = tgt[...] == t_iota
-    first = jnp.min(jnp.where(match, b_iota, 127), axis=1, keepdims=True)
-    last = jnp.max(jnp.where(match, b_iota, 0), axis=1, keepdims=True)
-    slot_v[...] = jnp.where(b_iota == 0, first, last)
-    cp_slot = pltpu.make_async_copy(slot_v, slot_s, in_sem.at[4])
-    cp_slot.start()
-    def send_blocks(dz, dx):
-        to = ((z + dz + ZN) % ZN) * XN + (x + dx) % XN
-        remote(
-            packed.at[pl.ds(2 * to, 2)], rel_ref.at[mine], a2a_send, a2a_recv, {"ctx": to}
-        ).start()
-
-    def bulk(slot):
-        for shifts, low, high in PLAN[slot]:
-
-            def one(dx, carry):
-                for dz in shifts:
-                    send_blocks(dz, dx)
-                return carry
-
-            lax.fori_loop(low, high, one, 0)
-
-    def far_first(send):
-        def both_ways(step, carry):
-            send(ZN // 2 + step)
-            send(ZN // 2 - step)
-            return carry
-
-        send(ZN // 2)
-        lax.fori_loop(1, ZN // 2, both_ways, 0)
 
     cp_slot.wait()
     cp_cache.wait()

time: 71.7 us -> 72.5 us (1.011)
  no operation moved by 1% of the time
where the time goes in v6:
time: 72.5 us; the launch traced here: 71.4 us
  Pallas kernels  69.2 us (95%)
  local copies, waits for them, and re-layouts  1.55 us (2%)
    pallas_call x1, Pallas kernels, body(): pl.pallas_call(kernel, out_shape=(pltpu.VMEM((3, 4, 128), bf16), pltpu.VM...  69.2 us
    unnamed x2, local copies, waits for them, and re-layouts  1.55 us

profile of v6, /device:TPU:24, one launch (start us, length us, event | category | flops | bytes accessed | tf_op | source)
XLA Modules:
  0.0 71.4 jit_solution(18043907342111497098)
XLA Ops:
  0.6 69.2 %decode_and_relay.1 = (bf16[3,4,128]{2,1,0:T(4,128)(2,1)S(1)}, bf16[128,16,256]{2,1,0:T(8,128)(2,1)S(1)}) custom-call(s32[4]{0:T(128)} %len_ref.1, bf16[3,4,128]{2,1,0:T(4,128)(2,1)} %hid_hbm.1, f32[1,128]{1,0:T(1,128)} %bitcast.14, f32[1,128]{1,0:T(1,128)} %constant.2.clone.inv_hbm, s32[1,64]{1,0:T(1,128)} %bitcast.15, s32[64,1,128]{2,1,0:T(1,128)} %bitcast.13, ...), custom_call_target="tpu_custom_call" | custom-call | tf_op jit(solution)/shard_map/decode_and_relay/pallas_call | solution.py:415
  69.9 0.6 copy.14
  70.5 1.0 %copy.15 = bf16[128,16,1,256]{3,1,2,0:T(8,128)(2,1)} copy(bf16[128,16,1,256]{3,1,2,0:T(8,128)(2,1)S(1)} %bitcast.9) | data formatting | bytes 2097152
